TPU v7x, 256 devices: a whole 4x4x8 slice. The times are simulated.
256 devices in a mesh: rep: 4 (over z_hi, core), fsdp: 64 (over x, y, z_lo).
Axes of the slice: x: 4, y: 4, z: 8 (z_hi: 2, z_lo: 4; z = z_hi * 4 + z_lo), core: 2. Of those that a mesh axis runs over, the one named last changes fastest.
Arguments:
- base_weights: float32 [4096, 14336], P('fsdp'), may hold values from -4 to 4
- local_weights: bfloat16 [4, 4096, 14336], P('rep', 'fsdp'), may hold values from -4 to 4
- momentum: float32 [4096, 14336], P('fsdp', 'rep'), may hold values from -3 to 3
- drift_exponent: int32 [4, 4096, 112], P('rep', 'fsdp'), may hold values from -3 to -1
- sum_exponent: int32 [4096, 112], P('fsdp', 'rep'), may hold values from -3 to -1
- blend_ratio: int32 [2], replicated, may hold values from 1 to 8, as said below
Outputs:
- new_base: float32 [4096, 14336], P('fsdp')
- new_momentum: float32 [4096, 14336], P('fsdp', 'rep')
- new_local: bfloat16 [4, 4096, 14336], P('rep', 'fsdp')
Inputs may be any that keep to these rules, and one draw needn't show every extreme that they name: blend_ratio[1] is 8 and blend_ratio[0] < blend_ratio[1].
All inputs are finite; a program needn't handle non-finite values.
Results may differ from a plain program's by a relative error of at most 0.0029.
Values may be sent and summed in bfloat16 or wider, within the bound.
No kernel may reach another device: no remote copies, remote signals or barrier semaphores. Data moves between devices by JAX's collectives and lax.ppermute only.
A program may use at most 64 MiB of HBM per device.

v0:
```python
import jax
import jax.numpy as jnp
from jax import lax
from jax.sharding import PartitionSpec as P

BLOCK = 128


momentum_decay = 0.9
outer_rate = 0.7


def block_scales(exponent):
    table = jnp.zeros(exponent.shape, jnp.float32)
    for exponent_value in range(-8, 1):
        table = jnp.where(exponent == exponent_value, jnp.float32(2.0**exponent_value), table)
    return table


def block_codes(values, exponent):
    shape = values.shape
    blocks = values.reshape(shape[:-1] + (shape[-1] // BLOCK, BLOCK))
    scales = block_scales(exponent)[..., None]
    levels = jnp.clip(jnp.floor(blocks / scales + 0.5), -8.0, 7.0)
    return (levels * scales).reshape(shape)


def on_device(base_weights, local_weights, momentum, drift_exponent, sum_exponent, blend_ratio):
    replicas = lax.axis_size("rep")
    cols_owned = momentum.shape[1]
    drift = base_weights - local_weights[0].astype(jnp.float32)
    sent = block_codes(drift, drift_exponent[0]).astype(jnp.bfloat16)
    summed = lax.psum_scatter(
        sent.astype(jnp.float32).astype(jnp.bfloat16), "rep", scatter_dimension=1, tiled=True
    ).astype(jnp.float32)
    outer_grad = block_codes(summed / replicas, sum_exponent)
    new_momentum = momentum_decay * momentum + outer_grad
    owned_base = lax.dynamic_slice_in_dim(
        base_weights, lax.axis_index("rep") * cols_owned, cols_owned, 1
    )
    owned_new = owned_base - outer_rate * (outer_grad + momentum_decay * new_momentum)
    new_base = lax.all_gather(owned_new, "rep", axis=1, tiled=True)
    share = blend_ratio[0].astype(jnp.float32) / blend_ratio[1].astype(jnp.float32)
    new_local = (share * local_weights.astype(jnp.float32) + (1.0 - share) * new_base[None]).astype(
        jnp.bfloat16
    )
    return (new_base, new_momentum, new_local)


def solution(mesh):
    return jax.shard_map(
        on_device,
        mesh=mesh,
        in_specs=(
            P("fsdp", None),
            P("rep", "fsdp", None),
            P("fsdp", "rep"),
            P("rep", "fsdp", None),
            P("fsdp", "rep"),
            P(),
        ),
        out_specs=(P("fsdp", None), P("fsdp", "rep"), P("rep", "fsdp", None)),
        check_vma=False,
    )
```

profile of v0, /device:TPU:35, one launch (start us, length us, event | category | flops | bytes accessed | tf_op | source)
XLA Modules:
  0.0 144.6 jit_solution(9861805775487084473)
XLA Ops:
  7.2 0.0 copy-start.1
  7.2 0.0 reduce-scatter.2.cloned.1.call-start
  7.2 0.9 select_bitcast_fusion
  8.1 1.0 div.34
  9.1 0.0 copy-done.1
  9.1 0.0 copy-start.3
  9.2 0.0 copy-start.2
  9.2 5.4 %fusion.8 = bf16[64,14336]{1,0:T(8,128)(2,1)} fusion(f32[8,8,112,128]{3,2,1,0:T(8,128)S(1)} %bitcast.43, f32[64,14336]{1,0:T(8,128)} %param.6, bf16[1,64,14336]{2,1,0:T(8,128)(2,1)S(1)} %copy-done.1), kind=kLoop, calls=%fused_computation.10 | loop fusion | flops 7340032 | bytes 11010048 | tf_op jit(solution)/shard_map/convert_element_type | solution.py:32
  14.5 0.0 reduce-scatter.2.cloned.1.call-update
  14.5 0.0 copy-start.4
  14.6 0.0 all-gather.2.cloned.1.call-start
  14.6 0.0 copy-done.3
  14.6 0.1 copy.10
  14.7 56.2 %reduce-scatter.2.cloned.1.call-done = bf16[64,3584]{1,0:T(8,128)(2,1)} async-done(((bf16[64,14336]{1,0:T(8,128)(2,1)}), bf16[64,3584]{1,0:T(8,128)(2,1)}) %reduce-scatter.2.cloned.1.call-update) | async-done | bytes 458768 | tf_op jit(solution)/shard_map/reduce_scatter | solution.py:33
  71.0 0.3 div.39
  71.3 0.0 copy-done.2
  71.3 3.5 %multiply_subtract_fusion = (f32[64,3584]{1,0:T(8,128)}, f32[64,3584]{1,0:T(8,128)}) fusion(f32[64,14336]{1,0:T(8,128)} %param.6, s32[]{:T(128)S(6)} %select_n.100, f32[8,8,28,128]{3,2,1,0:T(8,128)S(1)} %bitcast.44, bf16[64,3584]{1,0:T(8,128)(2,1)} %reduce-scatter.2.cloned.1.call-done, f32[64,3584]{1,0:T(8,128)S(1)} %copy-done.2), kind=kLoop, calls=%fused_computation.16 | loop fusion | flops 2981888 | bytes 5046276 | tf_op jit(solution)/shard_map/sub | solution.py:41
  74.8 0.0 all-gather.2.cloned.1.call-update
  74.8 0.0 copy-done.4
  74.8 0.6 fusion.12
  76.7 55.3 %all-gather.2.cloned.1.call-done = f32[64,14336]{1,0:T(8,128)} async-done(((f32[64,3584]{1,0:T(8,128)}), f32[64,14336]{1,0:T(8,128)}) %all-gather.2.cloned.1.call-update) | async-done | bytes 3670032 | tf_op jit(solution)/shard_map/all_gather | solution.py:42
  132.0 0.0 copy-start
  132.0 4.0 %fusion.7 = bf16[1,64,14336]{2,1,0:T(8,128)(2,1)} fusion(bf16[1,64,14336]{2,1,0:T(8,128)(2,1)S(1)} %copy-done.1, f32[64,14336]{1,0:T(8,128)} %all-gather.2.cloned.1.call-done, f32[]{:T(128)S(6)} %sub.11, f32[]{:T(128)} %bitcast.2), kind=kLoop, calls=%fused_computation.9 | loop fusion | flops 4587520 | bytes 7340040 | tf_op jit(solution)/shard_map/convert_element_type | solution.py:44
  135.9 0.0 copy-done
  135.9 1.8 %copy.23 = f32[64,14336]{1,0:T(8,128)} copy(f32[64,14336]{1,0:T(8,128)S(1)} %copy-done) | data formatting | bytes 7340032
  (1 shorter events, 0.0 us)
Async XLA Ops:
  7.2 2.0 %copy-start.1 = (bf16[1,64,14336]{2,1,0:T(8,128)(2,1)S(1)}, bf16[1,64,14336]{2,1,0:T(8,128)(2,1)}, u32[]{:S(2)}) copy-start(bf16[1,64,14336]{2,1,0:T(8,128)(2,1)} %param.7) | copy-start | bytes 5505028
  7.2 63.8 %reduce-scatter.2.cloned.1.call-start = ((), (), s32[]{:S(2)}) async-start(), calls=%async_computation.1 | async-start | bytes 2293760 | tf_op jit(solution)/shard_map/reduce_scatter | solution.py:33
  9.1 5.5 %copy-start.3 = (s32[64,28]{0,1:T(8,128)S(1)}, s32[64,28]{0,1:T(8,128)}, u32[]{:S(2)}) copy-start(s32[64,28]{0,1:T(8,128)} %param.10) | copy-start | bytes 21508
  9.2 62.1 %copy-start.2 = (f32[64,3584]{1,0:T(8,128)S(1)}, f32[64,3584]{1,0:T(8,128)}, u32[]{:S(2)}) copy-start(f32[64,3584]{1,0:T(8,128)} %param.8) | copy-start | bytes 2752516
  14.5 60.3 %copy-start.4 = (s32[2]{0:T(128)S(1)}, s32[2]{0:T(128)}, u32[]{:S(2)}) copy-start(s32[2]{0:T(128)} %param.11) | copy-start | bytes 28
  14.6 117.4 %all-gather.2.cloned.1.call-start = ((), (), s32[]{:S(2)}) async-start(), calls=%async_computation.2 | async-start | bytes 4587520 | tf_op jit(solution)/shard_map/all_gather | solution.py:42
  132.0 4.0 %copy-start = (f32[64,14336]{1,0:T(8,128)S(1)}, f32[64,14336]{1,0:T(8,128)}, u32[]{:S(2)}) copy-start(f32[64,14336]{1,0:T(8,128)} %all-gather.2.cloned.1.call-done) | copy-start | bytes 11010052
Sparse Core Ops, SparseCore 0:
  14.7 56.2 reduce-scatter.1
  74.9 56.9 all-gather.1
where the time goes:
time: 147 us; the launch traced here: 145 us
  waiting for transfers between devices  112 us (76%)
  between operations  15.4 us (10%)
  other arithmetic  13.7 us (9%)
  local copies, waits for them, and re-layouts  3.87 us (3%)
    reduce_scatter x1, waiting for transfers between devices, on_device(): lax.psum_scatter(sent.astype(jnp.float32).astype(jnp.bfloat16), 'rep', sc...  56.2 us
    all_gather x1, waiting for transfers between devices, on_device(): new_base = lax.all_gather(owned_new, 'rep', axis=1, tiled=True)  55.3 us
    convert_element_type x1, other arithmetic, on_device(): sent = block_codes(drift, drift_exponent[0]).astype(jnp.bfloat16)  5.35 us
    convert_element_type x1, other arithmetic, on_device(): (share * local_weights.astype(jnp.float32) + (1.0 - share) * new_base[Non...  3.95 us
    sub x1, other arithmetic, on_device(): owned_base - outer_rate * (outer_grad + momentum_decay * new_momentum)  3.49 us
  transfers between devices with their start and end apart: 2, of which 2 were waited for; matrix products, arithmetic and copies ran while one was open for 0% of the time, Pallas kernels for 0%

commit v1 on v0

v1 whole, which is shorter than its diff:
```python
import functools

import jax
import jax.numpy as jnp
from jax import lax
from jax.experimental import pallas as pl
from jax.experimental.pallas import tpu as pltpu
from jax.sharding import PartitionSpec as P

BLOCK = 128
QUARTER = 28
CHUNKS = (15, 13)
PIECE = 7

VMEM_LIMIT = 12 * 1024 * 1024

momentum_decay = 0.9
outer_rate = 0.7

F32 = jnp.float32
BF16 = jnp.bfloat16
IN_HBM = pl.BlockSpec(memory_space=pltpu.HBM)
ANYWHERE = pl.BlockSpec(memory_space=pl.ANY)
IN_VMEM = pl.BlockSpec(memory_space=pltpu.VMEM)


class Copies:
    def __init__(self, sems):
        self.sems = sems
        self.used = 0

    def start(self, source, target):
        copy = pltpu.make_async_copy(source, target, self.sems.at[self.used])
        self.used += 1
        copy.start()
        return copy


def pieces_of(blocks):
    return [(i, min(PIECE, blocks - i)) for i in range(0, blocks, PIECE)]


def window(quarter, start, count):
    return pl.ds(pl.multiple_of((quarter * QUARTER + start) * BLOCK, BLOCK), count * BLOCK)


def span(start, count):
    return pl.ds(start * BLOCK, count * BLOCK)


def scale_table(exponent):
    rows, blocks = exponent.shape
    if blocks < BLOCK:
        exponent = jnp.concatenate([exponent, jnp.zeros((rows, BLOCK - blocks), jnp.int32)], 1)
    scale = jnp.zeros(exponent.shape, F32)
    inverse = jnp.zeros(exponent.shape, F32)
    for value in range(-8, 1):
        hit = exponent == value
        scale = jnp.where(hit, F32(2.0**value), scale)
        inverse = jnp.where(hit, F32(2.0**-value), inverse)
    return scale, inverse


def rolled(table, first):
    return tuple(pltpu.roll(x, lax.rem(BLOCK - first, BLOCK), 1) for x in table)


def code(values, scales, j):
    scale, inverse = (s[:, j : j + 1] for s in scales)
    return jnp.clip(jnp.floor(values * inverse + 0.5), -8.0, 7.0) * scale


def block(j):
    return slice(j * BLOCK, (j + 1) * BLOCK)


def codes_kernel(parts, n_after, base, local, drift, *refs):
    outs = refs[n_after : n_after + len(parts)]
    base_at, local_at, drift_at, sems = refs[n_after + len(parts) :]
    rep = lax.axis_index("rep")
    copies = Copies(sems)
    exps = copies.start(drift, drift_at)
    arriving = []
    at = 0
    for out, (flip, start, count) in zip(outs, parts):
        for i, n in pieces_of(count):
            cols, here = window(rep ^ flip, start + i, n), span(at, n)
            arriving.append((
                out, i, n, at, (rep ^ flip) * QUARTER + start + i,
                copies.start(base.at[:, cols], base_at.at[:, here]),
                copies.start(local.at[0, :, cols], local_at.at[:, here]),
            ))
            at += n
    exps.wait()
    table = scale_table(drift_at[0])
    for out, i, n, at, first, *group in arriving:
        scales = rolled(table, first)
        for copy in group:
            copy.wait()
        for j in range(n):
            cols = block(at + j)
            drifted = base_at[:, cols] - local_at[:, cols].astype(F32)
            out[:, block(i + j)] = code(drifted, scales, j).astype(BF16)


def pair_kernel(n_after, own, other, *refs):
    out = refs[n_after]
    for j in range(own.shape[1] // BLOCK):
        cols = block(j)
        out[:, cols] = (own[:, cols].astype(F32) + other[:, cols].astype(F32)).astype(BF16)


def update_kernel(start, count, n_others, first, base, local, drift, sums, momentum, share, remote, *refs):
    others, refs = refs[:n_others], refs[n_others:]
    others = [(ref, j) for ref in others for j in range(ref.shape[1] // BLOCK)]
    if not first:
        refs = refs[3:]
    new_base, new_momentum, new_local, sent, kept = refs[:5]
    base_at, local_at, drift_at, sums_at, momentum_at, share_at = refs[5:11]
    out_base, out_momentum, out_local, sems, out_sems = refs[11:]
    quarter = lax.axis_index("rep")
    copies, leaving = Copies(sems), Copies(out_sems)
    small = [copies.start(drift, drift_at), copies.start(sums, sums_at), copies.start(share, share_at)]
    arriving = []
    for i, n in pieces_of(count):
        cols, here = window(quarter, start + i, n), span(i, n)
        arriving.append([
            copies.start(base.at[:, cols], base_at.at[:, here]),
            copies.start(local.at[0, :, cols], local_at.at[:, here]),
            copies.start(momentum.at[:, span(start + i, n)], momentum_at.at[:, here]),
        ])
    for copy in small:
        copy.wait()
    scales = rolled(scale_table(drift_at[0]), quarter * QUARTER + start)
    sum_scales = scale_table(sums_at[...])
    part = share_at[0:1, :]
    outs = []
    for (i, n), group in zip(pieces_of(count), arriving):
        for copy in group:
            copy.wait()
        for j in range(i, i + n):
            cols = block(j)
            old = base_at[:, cols]
            layer = local_at[:, cols].astype(F32)
            own = code(old - layer, scales, j)
            other, at = others[j]
            summed = own + other[:, block(at)].astype(F32) + remote[:, cols].astype(F32)
            outer_grad = code(summed * 0.25, sum_scales, start + j)
            moved = momentum_decay * momentum_at[:, cols] + outer_grad
            value = old - outer_rate * (outer_grad + momentum_decay * moved)
            rounded = value.astype(BF16)
            out_momentum[:, cols] = moved
            kept[:, cols] = value
            sent[:, cols] = rounded
            out_base[:, cols] = rounded.astype(F32)
            out_local[:, cols] = (part * layer + (1.0 - part) * value).astype(BF16)
        cols, here = window(quarter, start + i, n), span(i, n)
        outs += [
            leaving.start(out_base.at[:, here], new_base.at[:, cols]),
            leaving.start(out_momentum.at[:, here], new_momentum.at[:, span(start + i, n)]),
            leaving.start(out_local.at[:, here], new_local.at[0, :, cols]),
        ]
    for copy in outs:
        copy.wait()


def blend_kernel(parts, n_values, local, share, *refs):
    values = refs[:n_values]
    new_base, new_local = refs[n_values + 2 : n_values + 4]
    local_at, share_at, out_base, out_local, sems, out_sems = refs[n_values + 4 :]
    rep = lax.axis_index("rep")
    copies, leaving = Copies(sems), Copies(out_sems)
    shared = copies.start(share, share_at)
    arriving = []
    places = []
    at = 0
    for value, (flip, start, count) in zip(values, parts):
        for i, n in pieces_of(count):
            cols, here = window(rep ^ flip, start + i, n), span(at, n)
            places.append((value, i, at, n, cols, here))
            arriving.append(copies.start(local.at[0, :, cols], local_at.at[:, here]))
            at += n
    shared.wait()
    part = share_at[0:1, :]
    outs = []
    for (value, i, at, n, cols, here), copy in zip(places, arriving):
        copy.wait()
        for j in range(n):
            layer = local_at[:, block(at + j)].astype(F32)
            arrived = value[:, block(i + j)].astype(F32)
            out_base[:, block(at + j)] = arrived.astype(BF16).astype(F32)
            out_local[:, block(at + j)] = (part * layer + (1.0 - part) * arrived).astype(BF16)
        outs += [
            leaving.start(out_base.at[:, here], new_base.at[:, cols]),
            leaving.start(out_local.at[:, here], new_local.at[0, :, cols]),
        ]
    for copy in outs:
        copy.wait()


def on_device(base_weights, local_weights, momentum, drift_exponent, sum_exponent, blend_ratio):
    plain_local = local_weights
    base_weights, local_weights, momentum, drift_exponent = (
        pltpu.with_memory_space_constraint(x, pltpu.HBM)
        for x in (base_weights, local_weights, momentum, drift_exponent)
    )
    rows, cols = base_weights.shape
    owned = momentum.shape[1]
    blocks = drift_exponent.shape[2]
    sum_exponent = jnp.pad(sum_exponent, ((0, 0), (0, BLOCK - sum_exponent.shape[1])))
    share = blend_ratio[0].astype(F32) / blend_ratio[1].astype(F32)
    share = jnp.full((8, BLOCK), share, F32)

    def wide(count, dtype):
        return pltpu.VMEM((rows, count * BLOCK), dtype)

    def sems(n):
        return pltpu.SemaphoreType.DMA((n,))

    def call(body, in_specs, out_specs, out_shape, scratch, name, aliases=None, cost=1):
        return pl.pallas_call(
            body,
            in_specs=in_specs,
            out_specs=out_specs,
            out_shape=out_shape,
            scratch_shapes=scratch,
            input_output_aliases=aliases or {},
            compiler_params=pltpu.CompilerParams(vmem_limit_bytes=VMEM_LIMIT),
            cost_estimate=pl.CostEstimate(flops=1, bytes_accessed=cost, transcendentals=0),
            name=name,
        )

    def codes(parts, after=()):
        count = sum(p[2] for p in parts)
        n = sum(len(pieces_of(p[2])) for p in parts)
        return call(
            functools.partial(codes_kernel, parts, len(after)),
            [IN_HBM] * 3 + [ANYWHERE] * len(after), (IN_VMEM,) * len(parts),
            tuple(jax.ShapeDtypeStruct((rows, p[2] * BLOCK), BF16) for p in parts),
            [wide(count, F32), wide(count, BF16), pltpu.VMEM((1, rows, blocks), jnp.int32), sems(1 + 2 * n)],
            "codes",
        )(base_weights, local_weights, drift_exponent, *after)

    def pair(own, other, after=()):
        return call(
            functools.partial(pair_kernel, len(after)), [IN_VMEM] * 2 + [ANYWHERE] * len(after), IN_VMEM,
            jax.ShapeDtypeStruct(own.shape, BF16), [], "pair",
        )(own, other, *after)

    full = (
        jax.ShapeDtypeStruct((rows, cols), F32),
        jax.ShapeDtypeStruct((rows, owned), F32),
        jax.ShapeDtypeStruct((1, rows, cols), BF16),
    )

    def update(start, count, others, remote, held):
        n = len(pieces_of(count))
        args = [base_weights, local_weights, drift_exponent, sum_exponent, momentum, share, remote, *others]
        specs = [IN_HBM] * 3 + [ANYWHERE] + [IN_HBM] + [ANYWHERE] + [IN_VMEM] * (1 + len(others))
        aliases = {}
        if held is not None:
            aliases = {len(args) + i: i for i in range(3)}
            args += held
            specs += [IN_HBM] * 3
        out = call(
            functools.partial(update_kernel, start, count, len(others), held is None),
            specs, (IN_HBM,) * 3 + (IN_VMEM,) * 2,
            full + (
                jax.ShapeDtypeStruct((rows, count * BLOCK), BF16),
                jax.ShapeDtypeStruct((rows, count * BLOCK), F32),
            ),
            [
                wide(count, F32), wide(count, BF16), pltpu.VMEM((1, rows, blocks), jnp.int32),
                pltpu.VMEM((rows, BLOCK), jnp.int32), wide(count, F32), pltpu.VMEM((8, BLOCK), F32),
                wide(count, F32), wide(count, F32), wide(count, BF16), sems(3 + 3 * n), sems(3 * n),
            ],
            "update", aliases,
        )(*args)
        return list(out[:3]), out[3], out[4]

    def blend(parts, values, held, cost=1):
        count = sum(p[2] for p in parts)
        n = sum(len(pieces_of(p[2])) for p in parts)
        new_base, new_local = call(
            functools.partial(blend_kernel, parts, len(values)),
            [ANYWHERE] * 2 + [IN_VMEM] * len(values) + [IN_HBM] * 2, (IN_HBM, IN_HBM), (full[0], full[2]),
            [
                wide(count, BF16), pltpu.VMEM((8, BLOCK), F32),
                wide(count, F32), wide(count, BF16), sems(1 + n), sems(2 * n),
            ],
            "blend", {2 + len(values): 0, 3 + len(values): 1}, cost,
        )(plain_local, share, *values, held[0], held[2])
        return [new_base, held[1], new_local]

    def to_core(x):
        return lax.ppermute(x, "rep", [(0, 1), (1, 0), (2, 3), (3, 2)])

    def to_chip(x):
        return lax.ppermute(x, "rep", [(0, 2), (2, 0), (1, 3), (3, 1)])

    plan = [(sum(CHUNKS[:i]), CHUNKS[i]) for i in range(len(CHUNKS))]

    (a0, a1), (b0, b1) = plan
    there_first, here_first = codes([(3, a0, a1), (2, a0, a1)])
    there_second, here_second = codes([(3, b0, b1), (2, b0, b1)], after=(there_first,))
    core_first, core_second = to_core(there_first), to_core(there_second)
    pair_first = pair(here_first, core_first, after=(there_second,))
    pair_second = pair(here_second, core_second, after=(pair_first,))
    chip_first, chip_second = to_chip(pair_first), to_chip(pair_second)
    cuts = [(a0, a1 - a1 // 2), (a0 + a1 - a1 // 2, a1 // 2), (b0, b1 - b1 // 2), (b0 + b1 - b1 // 2, b1 // 2)]
    others = [to_core(x) for x in codes([(1, *cut) for cut in cuts], after=(pair_second,))]
    held, sent_first, kept_first = update(a0, a1, others[:2], chip_first, None)
    held, sent_second, kept_second = update(b0, b1, others[2:], chip_second, held)
    far_first, far_second = to_chip(sent_first), to_chip(sent_second)
    near_first, near_second = to_core(kept_first), to_core(kept_second)
    held = blend([(1, a0, a1), (1, b0, b1)], [near_first, near_second], held)
    held = blend([(2, a0, a1), (3, a0, a1)], [far_first, to_core(far_first)], held)
    far_second, held = lax.optimization_barrier((far_second, held))
    forwarded = to_core(far_second)
    held = blend([(2, b0, b1)], [far_second], held)
    held = blend([(3, b0, b1)], [forwarded], held)
    return tuple(held)


def solution(mesh):
    return jax.shard_map(
        on_device,
        mesh=mesh,
        in_specs=(
            P("fsdp", None),
            P("rep", "fsdp", None),
            P("fsdp", "rep"),
            P("rep", "fsdp", None),
            P("fsdp", "rep"),
            P(),
        ),
        out_specs=(P("fsdp", None), P("fsdp", "rep"), P("rep", "fsdp", None)),
        check_vma=False,
    )
```

time: 147 us -> 60.8 us (0.41); the launches traced: 145 us -> 60.6 us
  waiting for transfers between devices: 112 us -> 16.3 us
  starting transfers between devices: 0.08 us -> 25 us
  Pallas kernels: 0 us -> 16.5 us
  other arithmetic: 13.7 us -> 0 us
  between operations: 15.4 us -> 2.13 us
  local copies, waits for them, and re-layouts: 3.87 us -> 0.7 us
    reduce_scatter x1 -> x0, waiting for transfers between devices: 56.2 us -> none  [on_device(): lax.psum_scatter(sent.astype(jnp.float32).astype(jnp.bfloat16), 'rep', sc...]
    all_gather x1 -> x0, waiting for transfers between devices: 55.3 us -> none  [on_device(): new_base = lax.all_gather(owned_new, 'rep', axis=1, tiled=True)]
    ppermute x0 -> x14, starting transfers between devices: none -> 25 us  [the longest x4 18.5 us: to_chip(): return lax.ppermute(x, 'rep', [(0, 2), (2, 0), (1, 3), (3, 1)])]
    pallas_call x0 -> x11, Pallas kernels: none -> 16.5 us  [the longest x3 6.14 us: codes(): call(functools.partial(codes_kernel, parts, len(after)), [IN_HBM] * 3 + [...]
    ppermute x0 -> x14, waiting for transfers between devices: none -> 16.3 us  [the longest x4 16.1 us: to_chip(): return lax.ppermute(x, 'rep', [(0, 2), (2, 0), (1, 3), (3, 1)])]
    convert_element_type x2 -> x0, other arithmetic: 9.3 us -> none  [the longest x1 5.35 us: on_device(): sent = block_codes(drift, drift_exponent[0]).astype(jnp.bfloat16)]
    sub x1 -> x0, other arithmetic: 3.49 us -> none  [on_device(): owned_base - outer_rate * (outer_grad + momentum_decay * new_momentum)]
    unnamed x11 -> x7, local copies, waits for them, and re-layouts: 1.86 us -> 0.11 us
  transfers between devices with their start and end apart: 2 -> 14, of which waited for: 2 -> 4; matrix products, arithmetic and copies ran while one was open for 0% -> 1% of each run, Pallas kernels for 0% -> 22%
where the time goes in v1:
time: 60.8 us; the launch traced here: 60.6 us
  starting transfers between devices  25 us (41%)
  Pallas kernels  16.5 us (27%)
  waiting for transfers between devices  16.3 us (27%)
  between operations  2.13 us (4%)
  local copies, waits for them, and re-layouts  0.7 us (1%)
    ppermute x4, starting transfers between devices, to_chip(): return lax.ppermute(x, 'rep', [(0, 2), (2, 0), (1, 3), (3, 1)])  18.5 us
    ppermute x4, waiting for transfers between devices, to_chip(): return lax.ppermute(x, 'rep', [(0, 2), (2, 0), (1, 3), (3, 1)])  16.1 us
    ppermute x10, starting transfers between devices, to_core(): return lax.ppermute(x, 'rep', [(0, 1), (1, 0), (2, 3), (3, 2)])  6.53 us
    pallas_call x3, Pallas kernels, codes(): call(functools.partial(codes_kernel, parts, len(after)), [IN_HBM] * 3 + [...  6.14 us
    pallas_call x2, Pallas kernels, update(): call(functools.partial(update_kernel, start, count, len(others), held is...  5.58 us
    pallas_call x4, Pallas kernels, blend(): call(functools.partial(blend_kernel, parts, len(values)), [ANYWHERE] * 2...  4.6 us
  transfers between devices with their start and end apart: 14, of which 4 were waited for; matrix products, arithmetic and copies ran while one was open for 1% of the time, Pallas kernels for 22%

profile of v1, /device:TPU:35, one launch (start us, length us, event | category | flops | bytes accessed | tf_op | source)
XLA Modules:
  0.0 60.6 jit_solution(2909090800000593088)
XLA Ops:
  0.6 2.2 %codes.3 = (bf16[64,1920]{1,0:T(8,128)(2,1)S(1)}, bf16[64,1920]{1,0:T(8,128)(2,1)S(1)}) custom-call(f32[64,14336]{1,0:T(8,128)} %base.9, bf16[1,64,14336]{2,1,0:T(8,128)(2,1)} %local.17, s32[1,64,112]{2,1,0:T(8,128)} %drift.9), custom_call_target="tpu_custom_call" | custom-call | flops 1 | bytes 1 | tf_op jit(solution)/shard_map/codes/pallas_call | solution.py:236
  2.8 0.8 %collective-permute-start.1 = (bf16[64,1920]{1,0:T(8,128)(2,1)S(1)}, bf16[64,1920]{1,0:T(8,128)(2,1)S(1)}, u32[]{:S(2)}, u32[]{:S(2)}) collective-permute-start(bf16[64,1920]{1,0:T(8,128)(2,1)S(1)} %get-tuple-element.33.refs_0_), channel_id=1, source_target_pairs={{0,64},{64,0},{128,192},{192,128},{1,65},{65,1},{129,193},{193,129... | collective-permute-start | bytes 737288 | tf_op jit(solution)/shard_map/ppermute | solution.py:296
  3.6 1.9 %codes.4 = (bf16[64,1664]{1,0:T(8,128)(2,1)S(1)}, bf16[64,1664]{1,0:T(8,128)(2,1)S(1)}) custom-call(f32[64,14336]{1,0:T(8,128)} %base.9, bf16[1,64,14336]{2,1,0:T(8,128)(2,1)} %local.17, s32[1,64,112]{2,1,0:T(8,128)} %drift.9, bf16[64,1920]{1,0:T(8,128)(2,1)S(1)} %get-tuple-element.33.refs_0_), custom_call_target="tpu_custom_call" | custom-call | flops 1 | bytes 1 | tf_op jit(solution)/shard_map/codes/pallas_call | solution.py:236
  5.5 0.1 collective-permute-start
  5.6 0.0 copy-start.2
  5.6 0.1 pair.2.refs_0_
  5.7 6.1 %collective-permute-start.5 = (bf16[64,1920]{1,0:T(8,128)(2,1)S(1)}, bf16[64,1920]{1,0:T(8,128)(2,1)S(1)}, u32[]{:S(2)}, u32[]{:S(2)}) collective-permute-start(bf16[64,1920]{1,0:T(8,128)(2,1)S(1)} %pair.2.refs_0_), channel_id=1, source_target_pairs={{0,128},{128,0},{64,192},{192,64},{1,129},{129,1},{65,193},{193,65... | collective-permute-start | bytes 737288 | tf_op jit(solution)/shard_map/ppermute | solution.py:299
  11.8 0.1 pair.3.refs_0_
  11.9 2.0 %codes.5 = (bf16[64,1024]{1,0:T(8,128)(2,1)S(1)}, bf16[64,896]{1,0:T(8,128)(2,1)S(1)}, bf16[64,896]{1,0:T(8,128)(2,1)S(1)}, bf16[64,768]{1,0:T(8,128)(2,1)S(1)}) custom-call(f32[64,14336]{1,0:T(8,128)} %base.9, bf16[1,64,14336]{2,1,0:T(8,128)(2,1)} %local.17, s32[1,64,112]{2,1,0:T(8,128)} %drift.9, bf16[64,1664]{1,0:T(8,128)(2,1)S(1)} %pair.3.refs_0_), custom_call_target="tpu_custom_call" | custom-call | flops 1 | bytes 1 | tf_op jit(solution)/shard_map/codes/pallas_call | solution.py:236
  13.9 0.8 %collective-permute-start.7 = (bf16[64,896]{1,0:T(8,128)(2,1)S(1)}, bf16[64,896]{1,0:T(8,128)(2,1)S(1)}, u32[]{:S(2)}, u32[]{:S(2)}) collective-permute-start(bf16[64,896]{1,0:T(8,128)(2,1)S(1)} %get-tuple-element.40), channel_id=1, source_target_pairs={{0,64},{64,0},{128,192},{192,128},{1,65},{65,1},{129,193},{193,129... | collective-permute-start | bytes 344072 | tf_op jit(solution)/shard_map/ppermute | solution.py:296
  14.8 0.6 %collective-permute-start.2 = (bf16[64,1664]{1,0:T(8,128)(2,1)S(1)}, bf16[64,1664]{1,0:T(8,128)(2,1)S(1)}, u32[]{:S(2)}, u32[]{:S(2)}) collective-permute-start(bf16[64,1664]{1,0:T(8,128)(2,1)S(1)} %pair.3.refs_0_), channel_id=1, source_target_pairs={{0,128},{128,0},{64,192},{192,64},{1,129},{129,1},{65,193},{193,65... | collective-permute-start | bytes 638984 | tf_op jit(solution)/shard_map/ppermute | solution.py:299
  15.4 0.7 %collective-permute-start.6 = (bf16[64,1024]{1,0:T(8,128)(2,1)S(1)}, bf16[64,1024]{1,0:T(8,128)(2,1)S(1)}, u32[]{:S(2)}, u32[]{:S(2)}) collective-permute-start(bf16[64,1024]{1,0:T(8,128)(2,1)S(1)} %get-tuple-element.39), channel_id=1, source_target_pairs={{0,64},{64,0},{128,192},{192,128},{1,65},{65,1},{129,193},{193,129... | collective-permute-start | bytes 393224 | tf_op jit(solution)/shard_map/ppermute | solution.py:296
  16.1 0.5 collective-permute-start.3
  16.6 0.6 fusion
  18.5 0.1 copy.20
  18.6 5.4 %collective-permute-done.5.remote = bf16[64,1920]{1,0:T(8,128)(2,1)S(1)} collective-permute-done((bf16[64,1920]{1,0:T(8,128)(2,1)S(1)}, bf16[64,1920]{1,0:T(8,128)(2,1)S(1)}, u32[]{:S(2)}, u32[]{:S(2)}) %collective-permute-start.5) | collective-permute-done | bytes 245792 | tf_op jit(solution)/shard_map/ppermute | solution.py:299
  24.1 2.8 %update.2 = (f32[64,14336]{1,0:T(8,128)}, f32[64,3584]{1,0:T(8,128)}, bf16[1,64,14336]{2,1,0:T(8,128)(2,1)}, bf16[64,1920]{1,0:T(8,128)(2,1)S(1)}, f32[64,1920]{1,0:T(8,128)S(1)}) custom-call(f32[64,14336]{1,0:T(8,128)} %base.9, bf16[1,64,14336]{2,1,0:T(8,128)(2,1)} %local.17, s32[1,64,112]{2,1,0:T(8,128)} %drift.9, s32[64,128]{1,0:T(8,128)S(1)} %pad.4.sums, ...), custom_call_target="tpu_custom_call" | custom-call | flops 1 | bytes 1 | tf_op jit(solution)/shard_map/update/pallas_call | solution.py:265
  26.9 1.7 %collective-permute-start.11 = (f32[64,1920]{1,0:T(8,128)S(1)}, f32[64,1920]{1,0:T(8,128)S(1)}, u32[]{:S(2)}, u32[]{:S(2)}) collective-permute-start(f32[64,1920]{1,0:T(8,128)S(1)} %get-tuple-element.46), channel_id=1, source_target_pairs={{0,64},{64,0},{128,192},{192,128},{1,65},{65,1},{129,193},{193,129... | collective-permute-start | bytes 1474568 | tf_op jit(solution)/shard_map/ppermute | solution.py:296
  28.6 8.8 %collective-permute-start.9 = (bf16[64,1920]{1,0:T(8,128)(2,1)S(1)}, bf16[64,1920]{1,0:T(8,128)(2,1)S(1)}, u32[]{:S(2)}, u32[]{:S(2)}) collective-permute-start(bf16[64,1920]{1,0:T(8,128)(2,1)S(1)} %get-tuple-element.45), channel_id=1, source_target_pairs={{0,128},{128,0},{64,192},{192,64},{1,129},{129,1},{65,193},{193,65... | collective-permute-start | bytes 737288 | tf_op jit(solution)/shard_map/ppermute | solution.py:299
  37.4 0.0 copy-start
  37.4 2.8 %update.3 = (f32[64,14336]{1,0:T(8,128)}, f32[64,3584]{1,0:T(8,128)}, bf16[1,64,14336]{2,1,0:T(8,128)(2,1)}, bf16[64,1664]{1,0:T(8,128)(2,1)S(1)}, f32[64,1664]{1,0:T(8,128)S(1)}) custom-call(f32[64,14336]{1,0:T(8,128)} %base.9, bf16[1,64,14336]{2,1,0:T(8,128)(2,1)} %local.17, ...), custom_call_target="tpu_custom_call", output_to_operand_aliasing={{0}: (9, {}), {1}: (10, {}), {2}: (11, {})} | custom-call | flops 1 | bytes 1 | tf_op jit(solution)/shard_map/update/pallas_call | solution.py:265
  40.2 0.4 collective-permute-start.12
  40.7 5.4 %collective-permute-done.9.refs_0_ = bf16[64,1920]{1,0:T(8,128)(2,1)S(1)} collective-permute-done((bf16[64,1920]{1,0:T(8,128)(2,1)S(1)}, bf16[64,1920]{1,0:T(8,128)(2,1)S(1)}, u32[]{:S(2)}, u32[]{:S(2)}) %collective-permute-start.9) | collective-permute-done | bytes 245792 | tf_op jit(solution)/shard_map/ppermute | solution.py:299
  46.1 0.7 %collective-permute-start.10 = (bf16[64,1920]{1,0:T(8,128)(2,1)S(1)}, bf16[64,1920]{1,0:T(8,128)(2,1)S(1)}, u32[]{:S(2)}, u32[]{:S(2)}) collective-permute-start(bf16[64,1920]{1,0:T(8,128)(2,1)S(1)} %collective-permute-done.9.refs_0_), channel_id=1, source_target_pairs={{0,64},{64,0},{128,192},{192,128},{1,65},{65,1},{129,193},{193,129... | collective-permute-start | bytes 737288 | tf_op jit(solution)/shard_map/ppermute | solution.py:296
  46.8 2.9 %collective-permute-start.8 = (bf16[64,1664]{1,0:T(8,128)(2,1)S(1)}, bf16[64,1664]{1,0:T(8,128)(2,1)S(1)}, u32[]{:S(2)}, u32[]{:S(2)}) collective-permute-start(bf16[64,1664]{1,0:T(8,128)(2,1)S(1)} %get-tuple-element.44), channel_id=1, source_target_pairs={{0,128},{128,0},{64,192},{192,64},{1,129},{129,1},{65,193},{193,65... | collective-permute-start | bytes 638984 | tf_op jit(solution)/shard_map/ppermute | solution.py:299
  49.8 1.3 %blend.4 = (f32[64,14336]{1,0:T(8,128)}, bf16[1,64,14336]{2,1,0:T(8,128)(2,1)}) custom-call(bf16[1,64,14336]{2,1,0:T(8,128)(2,1)S(1)} %copy-done, f32[8,128]{1,0:T(8,128)S(1)} %broadcast_in_dim.3.share, f32[64,1920]{1,0:T(8,128)S(1)} %collective-permute-done.11.refs_0_, ...), custom_call_target="tpu_custom_call", output_to_operand_aliasing={{0}: (4, {}), {1}: (5, {})} | custom-call | flops 1 | bytes 1 | tf_op jit(solution)/shard_map/blend/pallas_call | solution.py:284
  51.1 1.4 %blend.5 = (f32[64,14336]{1,0:T(8,128)}, bf16[1,64,14336]{2,1,0:T(8,128)(2,1)}) custom-call(bf16[1,64,14336]{2,1,0:T(8,128)(2,1)S(1)} %copy-done, f32[8,128]{1,0:T(8,128)S(1)} %broadcast_in_dim.3.share, bf16[64,1920]{1,0:T(8,128)(2,1)S(1)} %collective-permute-done.9.refs_0_, ...), custom_call_target="tpu_custom_call", output_to_operand_aliasing={{0}: (4, {}), {1}: (5, {})} | custom-call | flops 1 | bytes 1 | tf_op jit(solution)/shard_map/blend/pallas_call | solution.py:284
  52.5 5.3 %collective-permute-done.8.refs_0_ = bf16[64,1664]{1,0:T(8,128)(2,1)S(1)} collective-permute-done((bf16[64,1664]{1,0:T(8,128)(2,1)S(1)}, bf16[64,1664]{1,0:T(8,128)(2,1)S(1)}, u32[]{:S(2)}, u32[]{:S(2)}) %collective-permute-start.8) | collective-permute-done | bytes 213024 | tf_op jit(solution)/shard_map/ppermute | solution.py:299
  57.8 0.7 %collective-permute-start.13 = (bf16[64,1664]{1,0:T(8,128)(2,1)S(1)}, bf16[64,1664]{1,0:T(8,128)(2,1)S(1)}, u32[]{:S(2)}, u32[]{:S(2)}) collective-permute-start(bf16[64,1664]{1,0:T(8,128)(2,1)S(1)} %collective-permute-done.8.refs_0_), channel_id=1, source_target_pairs={{0,64},{64,0},{128,192},{192,128},{1,65},{65,1},{129,193},{193,129... | collective-permute-start | bytes 638984 | tf_op jit(solution)/shard_map/ppermute | solution.py:296
  58.5 0.9 %blend.6 = (f32[64,14336]{1,0:T(8,128)}, bf16[1,64,14336]{2,1,0:T(8,128)(2,1)}) custom-call(bf16[1,64,14336]{2,1,0:T(8,128)(2,1)S(1)} %copy-done, f32[8,128]{1,0:T(8,128)S(1)} %broadcast_in_dim.3.share, bf16[64,1664]{1,0:T(8,128)(2,1)S(1)} %collective-permute-done.8.refs_0_, ...), custom_call_target="tpu_custom_call", output_to_operand_aliasing={{0}: (3, {}), {1}: (4, {})} | custom-call | flops 1 | bytes 1 | tf_op jit(solution)/shard_map/blend/pallas_call | solution.py:284
  59.5 0.1 collective-permute-done.13.refs_0_
  59.6 0.9 %blend.7 = (f32[64,14336]{1,0:T(8,128)}, bf16[1,64,14336]{2,1,0:T(8,128)(2,1)}) custom-call(bf16[1,64,14336]{2,1,0:T(8,128)(2,1)S(1)} %copy-done, f32[8,128]{1,0:T(8,128)S(1)} %broadcast_in_dim.3.share, bf16[64,1664]{1,0:T(8,128)(2,1)S(1)} %collective-permute-done.13.refs_0_, ...), custom_call_target="tpu_custom_call", output_to_operand_aliasing={{0}: (3, {}), {1}: (4, {})} | custom-call | flops 1 | bytes 1 | tf_op jit(solution)/shard_map/blend/pallas_call | solution.py:284
  (17 shorter events, 0.0 us)
Async XLA Ops:
  2.8 2.8 %collective-permute-start.1 = (bf16[64,1920]{1,0:T(8,128)(2,1)S(1)}, bf16[64,1920]{1,0:T(8,128)(2,1)S(1)}, u32[]{:S(2)}, u32[]{:S(2)}) collective-permute-start(bf16[64,1920]{1,0:T(8,128)(2,1)S(1)} %get-tuple-element.33.refs_0_), channel_id=1, source_target_pairs={{0,64},{64,0},{128,192},{192,128},{1,65},{65,1},{129,193},{193,129... | collective-permute-start | bytes 737288 | tf_op jit(solution)/shard_map/ppermute | solution.py:296
  5.5 6.3 %collective-permute-start = (bf16[64,1664]{1,0:T(8,128)(2,1)S(1)}, bf16[64,1664]{1,0:T(8,128)(2,1)S(1)}, u32[]{:S(2)}, u32[]{:S(2)}) collective-permute-start(bf16[64,1664]{1,0:T(8,128)(2,1)S(1)} %get-tuple-element.35.refs_0_), channel_id=1, source_target_pairs={{0,64},{64,0},{128,192},{192,128},{1,65},{65,1},{129,193},{193,129... | collective-permute-start | bytes 638984 | tf_op jit(solution)/shard_map/ppermute | solution.py:296
  5.6 11.0 %copy-start.2 = (s32[2]{0:T(128)S(1)}, s32[2]{0:T(128)}, u32[]{:S(2)}) copy-start(s32[2]{0:T(128)} %param.11) | copy-start | bytes 28
  5.6 12.8 %copy-start.1 = (s32[64,28]{0,1:T(8,128)S(1)}, s32[64,28]{0,1:T(8,128)}, u32[]{:S(2)}) copy-start(s32[64,28]{0,1:T(8,128)} %param.10) | copy-start | bytes 21508
  5.7 18.4 %collective-permute-start.5 = (bf16[64,1920]{1,0:T(8,128)(2,1)S(1)}, bf16[64,1920]{1,0:T(8,128)(2,1)S(1)}, u32[]{:S(2)}, u32[]{:S(2)}) collective-permute-start(bf16[64,1920]{1,0:T(8,128)(2,1)S(1)} %pair.2.refs_0_), channel_id=1, source_target_pairs={{0,128},{128,0},{64,192},{192,64},{1,129},{129,1},{65,193},{193,65... | collective-permute-start | bytes 737288 | tf_op jit(solution)/shard_map/ppermute | solution.py:299
  13.9 2.1 %collective-permute-start.7 = (bf16[64,896]{1,0:T(8,128)(2,1)S(1)}, bf16[64,896]{1,0:T(8,128)(2,1)S(1)}, u32[]{:S(2)}, u32[]{:S(2)}) collective-permute-start(bf16[64,896]{1,0:T(8,128)(2,1)S(1)} %get-tuple-element.40), channel_id=1, source_target_pairs={{0,64},{64,0},{128,192},{192,128},{1,65},{65,1},{129,193},{193,129... | collective-permute-start | bytes 344072 | tf_op jit(solution)/shard_map/ppermute | solution.py:296
  14.8 22.7 %collective-permute-start.2 = (bf16[64,1664]{1,0:T(8,128)(2,1)S(1)}, bf16[64,1664]{1,0:T(8,128)(2,1)S(1)}, u32[]{:S(2)}, u32[]{:S(2)}) collective-permute-start(bf16[64,1664]{1,0:T(8,128)(2,1)S(1)} %pair.3.refs_0_), channel_id=1, source_target_pairs={{0,128},{128,0},{64,192},{192,64},{1,129},{129,1},{65,193},{193,65... | collective-permute-start | bytes 638984 | tf_op jit(solution)/shard_map/ppermute | solution.py:299
  15.4 3.2 %collective-permute-start.6 = (bf16[64,1024]{1,0:T(8,128)(2,1)S(1)}, bf16[64,1024]{1,0:T(8,128)(2,1)S(1)}, u32[]{:S(2)}, u32[]{:S(2)}) collective-permute-start(bf16[64,1024]{1,0:T(8,128)(2,1)S(1)} %get-tuple-element.39), channel_id=1, source_target_pairs={{0,64},{64,0},{128,192},{192,128},{1,65},{65,1},{129,193},{193,129... | collective-permute-start | bytes 393224 | tf_op jit(solution)/shard_map/ppermute | solution.py:296
  16.1 21.4 %collective-permute-start.4 = (bf16[64,768]{1,0:T(8,128)(2,1)S(1)}, bf16[64,768]{1,0:T(8,128)(2,1)S(1)}, u32[]{:S(2)}, u32[]{:S(2)}) collective-permute-start(bf16[64,768]{1,0:T(8,128)(2,1)S(1)} %get-tuple-element.38), channel_id=1, source_target_pairs={{0,64},{64,0},{128,192},{192,128},{1,65},{65,1},{129,193},{193,129... | collective-permute-start | bytes 294920 | tf_op jit(solution)/shard_map/ppermute | solution.py:296
  16.1 21.3 %collective-permute-start.3 = (bf16[64,896]{1,0:T(8,128)(2,1)S(1)}, bf16[64,896]{1,0:T(8,128)(2,1)S(1)}, u32[]{:S(2)}, u32[]{:S(2)}) collective-permute-start(bf16[64,896]{1,0:T(8,128)(2,1)S(1)} %get-tuple-element.37), channel_id=1, source_target_pairs={{0,64},{64,0},{128,192},{192,128},{1,65},{65,1},{129,193},{193,129... | collective-permute-start | bytes 344072 | tf_op jit(solution)/shard_map/ppermute | solution.py:296
  26.9 22.9 %collective-permute-start.11 = (f32[64,1920]{1,0:T(8,128)S(1)}, f32[64,1920]{1,0:T(8,128)S(1)}, u32[]{:S(2)}, u32[]{:S(2)}) collective-permute-start(f32[64,1920]{1,0:T(8,128)S(1)} %get-tuple-element.46), channel_id=1, source_target_pairs={{0,64},{64,0},{128,192},{192,128},{1,65},{65,1},{129,193},{193,129... | collective-permute-start | bytes 1474568 | tf_op jit(solution)/shard_map/ppermute | solution.py:296
  28.6 17.5 %collective-permute-start.9 = (bf16[64,1920]{1,0:T(8,128)(2,1)S(1)}, bf16[64,1920]{1,0:T(8,128)(2,1)S(1)}, u32[]{:S(2)}, u32[]{:S(2)}) collective-permute-start(bf16[64,1920]{1,0:T(8,128)(2,1)S(1)} %get-tuple-element.45), channel_id=1, source_target_pairs={{0,128},{128,0},{64,192},{192,64},{1,129},{129,1},{65,193},{193,65... | collective-permute-start | bytes 737288 | tf_op jit(solution)/shard_map/ppermute | solution.py:299
  37.4 12.3 %copy-start = (bf16[1,64,14336]{2,1,0:T(8,128)(2,1)S(1)}, bf16[1,64,14336]{2,1,0:T(8,128)(2,1)}, u32[]{:S(2)}) copy-start(bf16[1,64,14336]{2,1,0:T(8,128)(2,1)} %local.17) | copy-start | bytes 5505028
  40.2 9.5 %collective-permute-start.12 = (f32[64,1664]{1,0:T(8,128)S(1)}, f32[64,1664]{1,0:T(8,128)S(1)}, u32[]{:S(2)}, u32[]{:S(2)}) collective-permute-start(f32[64,1664]{1,0:T(8,128)S(1)} %get-tuple-element.47), channel_id=1, source_target_pairs={{0,64},{64,0},{128,192},{192,128},{1,65},{65,1},{129,193},{193,129... | collective-permute-start | bytes 1277960 | tf_op jit(solution)/shard_map/ppermute | solution.py:296
  46.1 5.0 %collective-permute-start.10 = (bf16[64,1920]{1,0:T(8,128)(2,1)S(1)}, bf16[64,1920]{1,0:T(8,128)(2,1)S(1)}, u32[]{:S(2)}, u32[]{:S(2)}) collective-permute-start(bf16[64,1920]{1,0:T(8,128)(2,1)S(1)} %collective-permute-done.9.refs_0_), channel_id=1, source_target_pairs={{0,64},{64,0},{128,192},{192,128},{1,65},{65,1},{129,193},{193,129... | collective-permute-start | bytes 737288 | tf_op jit(solution)/shard_map/ppermute | solution.py:296
  46.8 11.0 %collective-permute-start.8 = (bf16[64,1664]{1,0:T(8,128)(2,1)S(1)}, bf16[64,1664]{1,0:T(8,128)(2,1)S(1)}, u32[]{:S(2)}, u32[]{:S(2)}) collective-permute-start(bf16[64,1664]{1,0:T(8,128)(2,1)S(1)} %get-tuple-element.44), channel_id=1, source_target_pairs={{0,128},{128,0},{64,192},{192,64},{1,129},{129,1},{65,193},{193,65... | collective-permute-start | bytes 638984 | tf_op jit(solution)/shard_map/ppermute | solution.py:299
  57.8 1.8 %collective-permute-start.13 = (bf16[64,1664]{1,0:T(8,128)(2,1)S(1)}, bf16[64,1664]{1,0:T(8,128)(2,1)S(1)}, u32[]{:S(2)}, u32[]{:S(2)}) collective-permute-start(bf16[64,1664]{1,0:T(8,128)(2,1)S(1)} %collective-permute-done.8.refs_0_), channel_id=1, source_target_pairs={{0,64},{64,0},{128,192},{192,128},{1,65},{65,1},{129,193},{193,129... | collective-permute-start | bytes 638984 | tf_op jit(solution)/shard_map/ppermute | solution.py:296

commit v2 on v1

v2 whole, which is shorter than its diff:
```python
import functools

import jax
import jax.numpy as jnp
from jax import lax
from jax.experimental import pallas as pl
from jax.experimental.pallas import tpu as pltpu
from jax.sharding import PartitionSpec as P

BLOCK = 128
QUARTER = 28
FIRST, SECOND = 16, 12
BACK_FIRST, BACK_SECOND = 13, 15
AWAY_SECOND = (12,)
CODES = (10, 9, 9)
NEAR_FIRST, NEAR_SECOND = (7, 6), (5, 5, 5)
FORWARD_FIRST = (7, 6)
PIECE = 7
VMEM_LIMIT = 12 * 1024 * 1024

momentum_decay = 0.9
outer_rate = 0.7

F32 = jnp.float32
BF16 = jnp.bfloat16
IN_HBM = pl.BlockSpec(memory_space=pltpu.HBM)
ANYWHERE = pl.BlockSpec(memory_space=pl.ANY)
IN_VMEM = pl.BlockSpec(memory_space=pltpu.VMEM)


class Copies:
    def __init__(self, sems):
        self.sems = sems
        self.used = 0

    def start(self, source, target):
        copy = pltpu.make_async_copy(source, target, self.sems.at[self.used])
        self.used += 1
        copy.start()
        return copy


def pieces_of(blocks):
    return [(i, min(PIECE, blocks - i)) for i in range(0, blocks, PIECE)]


def cut(start, counts):
    return [(start + sum(counts[:i]), count) for i, count in enumerate(counts)]


def window(quarter, start, count):
    return pl.ds(pl.multiple_of((quarter * QUARTER + start) * BLOCK, BLOCK), count * BLOCK)


def span(start, count):
    return pl.ds(start * BLOCK, count * BLOCK)


def block(j):
    return slice(j * BLOCK, (j + 1) * BLOCK)


def places_in(refs):
    return [(ref, j) for ref in refs for j in range(ref.shape[1] // BLOCK)]


def scale_table(exponent):
    rows, blocks = exponent.shape
    if blocks < BLOCK:
        exponent = jnp.concatenate([exponent, jnp.zeros((rows, BLOCK - blocks), jnp.int32)], 1)
    scale = jnp.zeros(exponent.shape, F32)
    inverse = jnp.zeros(exponent.shape, F32)
    for value in range(-8, 1):
        hit = exponent == value
        scale = jnp.where(hit, F32(2.0**value), scale)
        inverse = jnp.where(hit, F32(2.0**-value), inverse)
    return scale, inverse


def rolled(table, first):
    return tuple(pltpu.roll(x, lax.rem(BLOCK - first, BLOCK), 1) for x in table)


def code(values, scales, j):
    scale, inverse = (s[:, j : j + 1] for s in scales)
    return jnp.clip(jnp.floor(values * inverse + 0.5), -8.0, 7.0) * scale


def codes_kernel(parts, n_after, base, local, drift, *refs):
    outs = refs[n_after : n_after + len(parts)]
    base_at, local_at, drift_at, sems = refs[n_after + len(parts) :]
    rep = lax.axis_index("rep")
    copies = Copies(sems)
    exps = copies.start(drift, drift_at)
    arriving = []
    at = 0
    for out, (flip, start, count) in zip(outs, parts):
        for i, n in pieces_of(count):
            cols, here = window(rep ^ flip, start + i, n), span(at, n)
            arriving.append((
                out, i, n, at, (rep ^ flip) * QUARTER + start + i,
                copies.start(base.at[:, cols], base_at.at[:, here]),
                copies.start(local.at[0, :, cols], local_at.at[:, here]),
            ))
            at += n
    exps.wait()
    table = scale_table(drift_at[0])
    for out, i, n, at, first, *group in arriving:
        scales = rolled(table, first)
        for copy in group:
            copy.wait()
        for j in range(n):
            cols = block(at + j)
            drifted = base_at[:, cols] - local_at[:, cols].astype(F32)
            out[:, block(i + j)] = code(drifted, scales, j).astype(BF16)


def pair_kernel(own, *refs):
    *others, out = refs
    for j, (other, at) in enumerate(places_in(others)):
        cols = block(j)
        out[:, cols] = (own[:, cols].astype(F32) + other[:, block(at)].astype(F32)).astype(BF16)


def prepare_kernel(n_others, base, local, drift, momentum, sums, *refs):
    others = places_in(refs[:n_others])
    base_out, momentum_out, held, scale_out, inverse_out, local_at, drift_at, sems = refs[n_others:]
    quarter = lax.axis_index("rep")
    copies = Copies(sems)
    exps = copies.start(drift, drift_at)
    arriving = []
    for i, n in pieces_of(QUARTER):
        cols, here = window(quarter, i, n), span(i, n)
        arriving.append((
            copies.start(base.at[:, cols], base_out.at[:, here]),
            copies.start(local.at[0, :, cols], local_at.at[:, here]),
        ))
    last = copies.start(momentum, momentum_out)
    scale_out[...], inverse_out[...] = scale_table(sums[...])
    exps.wait()
    scales = rolled(scale_table(drift_at[0]), quarter * QUARTER)
    for (i, n), group in zip(pieces_of(QUARTER), arriving):
        for copy in group:
            copy.wait()
        for j in range(i, i + n):
            cols = block(j)
            other, at = others[j]
            own = code(base_out[:, cols] - local_at[:, cols].astype(F32), scales, j)
            held[:, cols] = (own + other[:, block(at)].astype(F32)).astype(BF16)
    last.wait()


def update_kernel(start, count, skip, n_remote, base, momentum, held, scale, inverse, *refs):
    remotes = places_in(refs[:n_remote])[skip:]
    sent, moved_out, *kept = refs[n_remote:]
    kept = places_in(kept)
    scales = scale[...], inverse[...]
    for j in range(count):
        cols, here = block(j), block(start + j)
        remote, at = remotes[j]
        summed = held[:, here].astype(F32) + remote[:, block(at)].astype(F32)
        outer_grad = code(summed * 0.25, scales, start + j)
        moved = momentum_decay * momentum[:, here] + outer_grad
        value = base[:, here] - outer_rate * (outer_grad + momentum_decay * moved)
        moved_out[:, cols] = moved
        sent[:, cols] = value.astype(BF16)
        keep, at = kept[j]
        keep[:, block(at)] = value


def blend_kernel(parts, n_values, n_moved, n_held, local, share, *refs):
    values = refs[:n_values]
    moved = refs[n_values : n_values + n_moved]
    refs = refs[n_values + n_moved + n_held :]
    new_base, new_local = refs[:2]
    out_base, out_local, sems = refs[-3:]
    rep = lax.axis_index("rep")
    leaving = Copies(sems)
    outs = []
    if n_moved:
        for ref, (start, count) in zip(moved, cut(0, [ref.shape[1] // BLOCK for ref in moved])):
            outs.append(leaving.start(ref, refs[2].at[:, span(start, count)]))
    part = share[0:1, :]
    at = 0
    for value, (flip, start, count) in zip(values, parts):
        for i, n in pieces_of(count):
            for j in range(n):
                layer = local[0, :, window(rep ^ flip, start + i + j, 1)].astype(F32)
                arrived = value[:, block(i + j)].astype(F32)
                out_base[:, block(at + j)] = arrived.astype(BF16).astype(F32)
                out_local[:, block(at + j)] = (part * layer + (1.0 - part) * arrived).astype(BF16)
            cols, here = window(rep ^ flip, start + i, n), span(at, n)
            outs += [
                leaving.start(out_base.at[:, here], new_base.at[:, cols]),
                leaving.start(out_local.at[:, here], new_local.at[0, :, cols]),
            ]
            at += n
    for copy in outs:
        copy.wait()


def on_device(base_weights, local_weights, momentum, drift_exponent, sum_exponent, blend_ratio):
    rows, cols = base_weights.shape
    owned = momentum.shape[1]
    blocks = drift_exponent.shape[2]
    sum_exponent = jnp.pad(sum_exponent, ((0, 0), (0, BLOCK - sum_exponent.shape[1])))
    share = blend_ratio[0].astype(F32) / blend_ratio[1].astype(F32)
    share = jnp.full((8, BLOCK), share, F32)
    in_hbm = [
        pltpu.with_memory_space_constraint(x, pltpu.HBM)
        for x in (base_weights, local_weights, drift_exponent, momentum)
    ]

    def wide(count, dtype):
        return pltpu.VMEM((rows, count * BLOCK), dtype)

    def sems(n):
        return pltpu.SemaphoreType.DMA((n,))

    def some(count, dtype):
        return jax.ShapeDtypeStruct((rows, count * BLOCK), dtype)

    def call(body, in_specs, out_specs, out_shape, scratch, name, aliases=None):
        return pl.pallas_call(
            body,
            in_specs=in_specs,
            out_specs=out_specs,
            out_shape=out_shape,
            scratch_shapes=scratch,
            input_output_aliases=aliases or {},
            compiler_params=pltpu.CompilerParams(vmem_limit_bytes=VMEM_LIMIT),
            cost_estimate=pl.CostEstimate(flops=1, bytes_accessed=1, transcendentals=0),
            name=name,
        )

    def codes(parts, after=()):
        count = sum(p[2] for p in parts)
        n = sum(len(pieces_of(p[2])) for p in parts)
        return call(
            functools.partial(codes_kernel, parts, len(after)),
            [IN_HBM] * 3 + [ANYWHERE] * len(after), (IN_VMEM,) * len(parts),
            tuple(some(p[2], BF16) for p in parts),
            [wide(count, F32), wide(count, BF16), pltpu.VMEM((1, rows, blocks), jnp.int32), sems(1 + 2 * n)],
            "codes",
        )(*in_hbm[:3], *after)

    def pair(own, others):
        return call(
            pair_kernel, [IN_VMEM] * (1 + len(others)), IN_VMEM, jax.ShapeDtypeStruct(own.shape, BF16), [], "pair",
        )(own, *others)

    def prepare(others):
        n = 2 * len(pieces_of(QUARTER)) + 2
        return call(
            functools.partial(prepare_kernel, len(others)),
            [IN_HBM] * 4 + [IN_VMEM] * (1 + len(others)), (IN_VMEM,) * 5,
            (some(QUARTER, F32), some(QUARTER, F32), some(QUARTER, BF16), some(1, F32), some(1, F32)),
            [wide(QUARTER, BF16), pltpu.VMEM((1, rows, blocks), jnp.int32), sems(n)], "prepare",
        )(*in_hbm, sum_exponent, *others)

    def update(start, count, skip, prepared, remotes, near):
        sent, moved, *kept = call(
            functools.partial(update_kernel, start, count, skip, len(remotes)), [IN_VMEM] * (5 + len(remotes)), (IN_VMEM,) * (2 + len(near)),
            (some(count, BF16), some(count, F32), *(some(n, F32) for n in near)), [], "update",
        )(*prepared, *remotes)
        return sent, moved, kept

    full = (
        jax.ShapeDtypeStruct((rows, cols), F32),
        jax.ShapeDtypeStruct((1, rows, cols), BF16),
        jax.ShapeDtypeStruct((rows, owned), F32),
    )

    def blend(parts, values, held=(), moved=()):
        count = sum(p[2] for p in parts)
        n = sum(len(pieces_of(p[2])) for p in parts)
        n_out = 3 if moved else 2
        at = 2 + len(values) + len(moved)
        return call(
            functools.partial(blend_kernel, parts, len(values), len(moved), len(held)),
            [IN_VMEM] * at + [IN_HBM] * len(held), (IN_HBM,) * n_out, full[:n_out],
            [wide(count, F32), wide(count, BF16), sems(2 * n + len(moved))],
            "blend", {at + i: i for i in range(len(held))},
        )(local_weights, share, *values, *moved, *held)

    def to_core(x):
        return lax.ppermute(x, "rep", [(0, 1), (1, 0), (2, 3), (3, 2)])

    def to_chip(x):
        return lax.ppermute(x, "rep", [(0, 2), (2, 0), (1, 3), (3, 1)])

    first, second = cut(0, (FIRST, SECOND))
    (there_first,) = codes([(3, *first)])
    here_first, *there_second = codes([(2, *first)] + [(3, *part) for part in cut(FIRST, AWAY_SECOND)], (there_first,))
    pair_first = pair(here_first, [to_core(there_first)])
    here_second, *mine = codes([(2, *second)] + [(1, *part) for part in cut(0, CODES)], (pair_first,))
    others = [to_core(x) for x in mine]
    pair_second = pair(here_second, [to_core(x) for x in there_second])
    chip_first, chip_second = to_chip(pair_first), to_chip(pair_second)
    prepared = prepare(others)
    first, second = cut(0, (BACK_FIRST, BACK_SECOND))
    sent_first, moved_first, kept_first = update(*first, 0, prepared, (chip_first,), NEAR_FIRST)
    remotes, skip = ((chip_first, chip_second), BACK_FIRST) if BACK_FIRST < FIRST else ((chip_second,), 0)
    sent_second, moved_second, kept_second = update(*second, skip, prepared, remotes, NEAR_SECOND)
    far_first, far_second = to_chip(sent_first), to_chip(sent_second)
    kept = [*kept_first, *kept_second]
    near = [to_core(x) for x in kept]
    pieces = cut(0, NEAR_FIRST + NEAR_SECOND)
    *held, new_momentum = blend(
        [(0, *part) for part in pieces] + [(1, *part) for part in pieces], kept + near,
        moved=(moved_first, moved_second),
    )
    pieces = cut(0, FORWARD_FIRST)
    forwarded = [to_core(lax.slice_in_dim(far_first, at * BLOCK, (at + n) * BLOCK, axis=1)) for at, n in pieces]
    held = blend([(2, *first)] + [(3, *piece) for piece in pieces], [far_first] + forwarded, held)
    far_second, held = lax.optimization_barrier((far_second, held))
    forwarded = to_core(far_second)
    held = blend([(2, *second)], [far_second], held)
    new_base, new_local = blend([(3, *second)], [forwarded], held)
    return new_base, new_momentum, new_local


def solution(mesh):
    return jax.shard_map(
        on_device,
        mesh=mesh,
        in_specs=(
            P("fsdp", None),
            P("rep", "fsdp", None),
            P("fsdp", "rep"),
            P("rep", "fsdp", None),
            P("fsdp", "rep"),
            P(),
        ),
        out_specs=(P("fsdp", None), P("fsdp", "rep"), P("rep", "fsdp", None)),
        check_vma=False,
    )
```

time: 60.8 us -> 56.9 us (0.936)
  Pallas kernels: 16.5 us -> 14 us
  waiting for transfers between devices: 16.3 us -> 14.6 us
    ppermute x4, waiting for transfers between devices: 16.1 us -> 13.4 us  [to_chip(): return lax.ppermute(x, 'rep', [(0, 2), (2, 0), (1, 3), (3, 1)])]
    pallas_call x8 -> x9, Pallas kernels: 10.3 us -> 7.75 us  [the longest x4 4.99 us: blend(): call(functools.partial(blend_kernel, parts, len(values), len(moved), len(...]
    ppermute x10 -> x13, starting transfers between devices: 6.53 us -> 8.23 us  [to_core(): return lax.ppermute(x, 'rep', [(0, 1), (1, 0), (2, 3), (3, 2)])]
    ppermute x4, starting transfers between devices: 18.5 us -> 17 us  [to_chip(): return lax.ppermute(x, 'rep', [(0, 2), (2, 0), (1, 3), (3, 1)])]
    ppermute x10 -> x13, waiting for transfers between devices: 0.17 us -> 1.21 us  [to_core(): return lax.ppermute(x, 'rep', [(0, 1), (1, 0), (2, 3), (3, 2)])]
  transfers between devices with their start and end apart: 14 -> 17, of which waited for: 4 -> 6; matrix products, arithmetic and copies ran while one was open for 1% -> 1% of each run, Pallas kernels for 22% -> 20%
where the time goes in v2:
time: 56.9 us; the launch traced here: 56.7 us
  starting transfers between devices  25.2 us (44%)
  waiting for transfers between devices  14.6 us (26%)
  Pallas kernels  14 us (25%)
  between operations  2.16 us (4%)
  local copies, waits for them, and re-layouts  0.72 us (1%)
    ppermute x4, starting transfers between devices, to_chip(): return lax.ppermute(x, 'rep', [(0, 2), (2, 0), (1, 3), (3, 1)])  17 us
    ppermute x4, waiting for transfers between devices, to_chip(): return lax.ppermute(x, 'rep', [(0, 2), (2, 0), (1, 3), (3, 1)])  13.4 us
    ppermute x13, starting transfers between devices, to_core(): return lax.ppermute(x, 'rep', [(0, 1), (1, 0), (2, 3), (3, 2)])  8.23 us
    pallas_call x3, Pallas kernels, codes(): call(functools.partial(codes_kernel, parts, len(after)), [IN_HBM] * 3 + [...  6.24 us
    pallas_call x4, Pallas kernels, blend(): call(functools.partial(blend_kernel, parts, len(values), len(moved), len(...  4.99 us
    pallas_call x1, Pallas kernels, prepare(): call(functools.partial(prepare_kernel, len(others)), [IN_HBM] * 4 + [IN_V...  1.94 us
    ppermute x13, waiting for transfers between devices, to_core(): return lax.ppermute(x, 'rep', [(0, 1), (1, 0), (2, 3), (3, 2)])  1.21 us
  transfers between devices with their start and end apart: 17, of which 6 were waited for; matrix products, arithmetic and copies ran while one was open for 1% of the time, Pallas kernels for 20%

profile of v2, /device:TPU:35, one launch (start us, length us, event | category | flops | bytes accessed | tf_op | source)
XLA Modules:
  0.0 56.7 jit_solution(5070608646983456574)
XLA Ops:
  0.6 1.6 %codes.3.refs_0_ = bf16[64,2048]{1,0:T(8,128)(2,1)S(1)} custom-call(f32[64,14336]{1,0:T(8,128)} %base.7, bf16[1,64,14336]{2,1,0:T(8,128)(2,1)} %local.15, s32[1,64,112]{2,1,0:T(8,128)} %drift.7), custom_call_target="tpu_custom_call" | custom-call | flops 1 | bytes 1 | tf_op jit(solution)/shard_map/codes/pallas_call | solution.py:239
  2.3 0.8 %collective-permute-start = (bf16[64,2048]{1,0:T(8,128)(2,1)S(1)}, bf16[64,2048]{1,0:T(8,128)(2,1)S(1)}, u32[]{:S(2)}, u32[]{:S(2)}) collective-permute-start(bf16[64,2048]{1,0:T(8,128)(2,1)S(1)} %codes.3.refs_0_), channel_id=1, source_target_pairs={{0,64},{64,0},{128,192},{192,128},{1,65},{65,1},{129,193},{193,129... | collective-permute-start | bytes 786440 | tf_op jit(solution)/shard_map/ppermute | solution.py:287
  3.0 2.0 %codes.4 = (bf16[64,2048]{1,0:T(8,128)(2,1)S(1)}, bf16[64,1536]{1,0:T(8,128)(2,1)S(1)}) custom-call(f32[64,14336]{1,0:T(8,128)} %base.7, bf16[1,64,14336]{2,1,0:T(8,128)(2,1)} %local.15, s32[1,64,112]{2,1,0:T(8,128)} %drift.7, bf16[64,2048]{1,0:T(8,128)(2,1)S(1)} %codes.3.refs_0_), custom_call_target="tpu_custom_call" | custom-call | flops 1 | bytes 1 | tf_op jit(solution)/shard_map/codes/pallas_call | solution.py:239
  5.1 0.1 collective-permute-start.5
  5.3 6.1 %collective-permute-start.4 = (bf16[64,2048]{1,0:T(8,128)(2,1)S(1)}, bf16[64,2048]{1,0:T(8,128)(2,1)S(1)}, u32[]{:S(2)}, u32[]{:S(2)}) collective-permute-start(bf16[64,2048]{1,0:T(8,128)(2,1)S(1)} %pair.2.refs_0_), channel_id=1, source_target_pairs={{0,128},{128,0},{64,192},{192,64},{1,129},{129,1},{65,193},{193,65... | collective-permute-start | bytes 786440 | tf_op jit(solution)/shard_map/ppermute | solution.py:290
  11.4 2.6 %codes.5 = (bf16[64,1536]{1,0:T(8,128)(2,1)S(1)}, bf16[64,1280]{1,0:T(8,128)(2,1)S(1)}, bf16[64,1152]{1,0:T(8,128)(2,1)S(1)}, bf16[64,1152]{1,0:T(8,128)(2,1)S(1)}) custom-call(f32[64,14336]{1,0:T(8,128)} %base.7, bf16[1,64,14336]{2,1,0:T(8,128)(2,1)} %local.15, s32[1,64,112]{2,1,0:T(8,128)} %drift.7, bf16[64,2048]{1,0:T(8,128)(2,1)S(1)} %pair.2.refs_0_), custom_call_target="tpu_custom_call" | custom-call | flops 1 | bytes 1 | tf_op jit(solution)/shard_map/codes/pallas_call | solution.py:239
  14.0 0.1 collective-permute-start.6
  14.1 0.8 %collective-permute-start.1 = (bf16[64,1280]{1,0:T(8,128)(2,1)S(1)}, bf16[64,1280]{1,0:T(8,128)(2,1)S(1)}, u32[]{:S(2)}, u32[]{:S(2)}) collective-permute-start(bf16[64,1280]{1,0:T(8,128)(2,1)S(1)} %get-tuple-element.36), channel_id=1, source_target_pairs={{0,64},{64,0},{128,192},{192,128},{1,65},{65,1},{129,193},{193,129... | collective-permute-start | bytes 491528 | tf_op jit(solution)/shard_map/ppermute | solution.py:287
  15.1 0.4 collective-permute-start.3
  15.6 0.8 %collective-permute-done.2.refs_1_ = bf16[64,1152]{1,0:T(8,128)(2,1)S(1)} collective-permute-done((bf16[64,1152]{1,0:T(8,128)(2,1)S(1)}, bf16[64,1152]{1,0:T(8,128)(2,1)S(1)}, u32[]{:S(2)}, u32[]{:S(2)}) %collective-permute-start.2) | collective-permute-done | bytes 147488 | tf_op jit(solution)/shard_map/ppermute | solution.py:287
  16.4 0.2 collective-permute-done.3.refs_2_
  16.6 1.9 %prepare.1 = (f32[64,3584]{1,0:T(8,128)S(1)}, f32[64,3584]{1,0:T(8,128)S(1)}, bf16[64,3584]{1,0:T(8,128)(2,1)S(1)}, f32[64,128]{1,0:T(8,128)S(1)}, f32[64,128]{1,0:T(8,128)S(1)}) custom-call(f32[64,14336]{1,0:T(8,128)} %base.7, bf16[1,64,14336]{2,1,0:T(8,128)(2,1)} %local.15, s32[1,64,112]{2,1,0:T(8,128)} %drift.7, f32[64,3584]{1,0:T(8,128)} %momentum.1, ...), custom_call_target="tpu_custom_call" | custom-call | flops 1 | bytes 1 | tf_op jit(solution)/shard_map/prepare/pallas_call | solution.py:254
  18.5 5.4 %collective-permute-done.4.refs_0_ = bf16[64,2048]{1,0:T(8,128)(2,1)S(1)} collective-permute-done((bf16[64,2048]{1,0:T(8,128)(2,1)S(1)}, bf16[64,2048]{1,0:T(8,128)(2,1)S(1)}, u32[]{:S(2)}, u32[]{:S(2)}) %collective-permute-start.4) | collective-permute-done | bytes 262176 | tf_op jit(solution)/shard_map/ppermute | solution.py:290
  24.0 0.3 update.3
  24.3 5.1 %collective-permute-start.8 = (bf16[64,1664]{1,0:T(8,128)(2,1)S(1)}, bf16[64,1664]{1,0:T(8,128)(2,1)S(1)}, u32[]{:S(2)}, u32[]{:S(2)}) collective-permute-start(bf16[64,1664]{1,0:T(8,128)(2,1)S(1)} %get-tuple-element.47), channel_id=1, source_target_pairs={{0,128},{128,0},{64,192},{192,64},{1,129},{129,1},{65,193},{193,65... | collective-permute-start | bytes 638984 | tf_op jit(solution)/shard_map/ppermute | solution.py:290
  29.4 4.9 %collective-permute-done.6.refs_1_ = bf16[64,1536]{1,0:T(8,128)(2,1)S(1)} collective-permute-done((bf16[64,1536]{1,0:T(8,128)(2,1)S(1)}, bf16[64,1536]{1,0:T(8,128)(2,1)S(1)}, u32[]{:S(2)}, u32[]{:S(2)}) %collective-permute-start.6) | collective-permute-done | bytes 196640 | tf_op jit(solution)/shard_map/ppermute | solution.py:290
  34.2 0.4 update.2
  34.6 3.9 %collective-permute-start.13 = (f32[64,640]{1,0:T(8,128)S(1)}, f32[64,640]{1,0:T(8,128)S(1)}, u32[]{:S(2)}, u32[]{:S(2)}) collective-permute-start(f32[64,640]{1,0:T(8,128)S(1)} %get-tuple-element.50.refs_2_), channel_id=1, source_target_pairs={{0,64},{64,0},{128,192},{192,128},{1,65},{65,1},{129,193},{193,129... | collective-permute-start | bytes 491528 | tf_op jit(solution)/shard_map/ppermute | solution.py:287
  38.6 0.4 collective-permute-start.15
  39.0 5.7 %collective-permute-start.7 = (bf16[64,1920]{1,0:T(8,128)(2,1)S(1)}, bf16[64,1920]{1,0:T(8,128)(2,1)S(1)}, u32[]{:S(2)}, u32[]{:S(2)}) collective-permute-start(bf16[64,1920]{1,0:T(8,128)(2,1)S(1)} %get-tuple-element.46), channel_id=1, source_target_pairs={{0,128},{128,0},{64,192},{192,64},{1,129},{129,1},{65,193},{193,65... | collective-permute-start | bytes 737288 | tf_op jit(solution)/shard_map/ppermute | solution.py:290
  44.7 0.4 collective-permute-start.11
  45.0 0.1 collective-permute-start.12
  45.2 0.4 collective-permute-start.9
  45.7 0.2 collective-permute-start.10
  45.9 0.6 %fusion = (s32[1]{0:T(128)}, s32[1]{0:T(128)}) fusion(s32[2]{0:T(128)S(1)} %copy-done.2), kind=kLoop, calls=%fused_computation | loop fusion | bytes 16 | tf_op jit(solution)/shard_map/slice | solution.py:207
  47.9 2.0 %blend.4 = (f32[64,14336]{1,0:T(8,128)}, bf16[1,64,14336]{2,1,0:T(8,128)(2,1)}, f32[64,3584]{1,0:T(8,128)}) custom-call(bf16[1,64,14336]{2,1,0:T(8,128)(2,1)S(1)} %copy-done, f32[8,128]{1,0:T(8,128)S(1)} %broadcast_in_dim.3.share, f32[64,896]{1,0:T(8,128)S(1)} %get-tuple-element.48.refs_0_, f32[64,768]{1,0:T(8,128)S(1)} %get-tuple-element.49.refs_1_, ...), custom_call_target="tpu_custom_call" | custom-call | flops 1 | bytes 1 | tf_op jit(solution)/shard_map/blend/pallas_call | solution.py:279
  49.9 1.1 %blend.5 = (f32[64,14336]{1,0:T(8,128)}, bf16[1,64,14336]{2,1,0:T(8,128)(2,1)}) custom-call(bf16[1,64,14336]{2,1,0:T(8,128)(2,1)S(1)} %copy-done, f32[8,128]{1,0:T(8,128)S(1)} %broadcast_in_dim.3.share, bf16[64,1664]{1,0:T(8,128)(2,1)S(1)} %collective-permute-done.8.refs_0_, ...), custom_call_target="tpu_custom_call", output_to_operand_aliasing={{0}: (5, {}), {1}: (6, {})} | custom-call | flops 1 | bytes 1 | tf_op jit(solution)/shard_map/blend/pallas_call | solution.py:279
  51.1 3.2 %collective-permute-done.7.refs_0_ = bf16[64,1920]{1,0:T(8,128)(2,1)S(1)} collective-permute-done((bf16[64,1920]{1,0:T(8,128)(2,1)S(1)}, bf16[64,1920]{1,0:T(8,128)(2,1)S(1)}, u32[]{:S(2)}, u32[]{:S(2)}) %collective-permute-start.7) | collective-permute-done | bytes 245792 | tf_op jit(solution)/shard_map/ppermute | solution.py:290
  54.2 0.4 collective-permute-start.16
  54.7 0.9 %blend.6 = (f32[64,14336]{1,0:T(8,128)}, bf16[1,64,14336]{2,1,0:T(8,128)(2,1)}) custom-call(bf16[1,64,14336]{2,1,0:T(8,128)(2,1)S(1)} %copy-done, f32[8,128]{1,0:T(8,128)S(1)} %broadcast_in_dim.3.share, bf16[64,1920]{1,0:T(8,128)(2,1)S(1)} %collective-permute-done.7.refs_0_, ...), custom_call_target="tpu_custom_call", output_to_operand_aliasing={{0}: (3, {}), {1}: (4, {})} | custom-call | flops 1 | bytes 1 | tf_op jit(solution)/shard_map/blend/pallas_call | solution.py:279
  55.6 0.2 collective-permute-done.16.refs_0_
  55.8 0.9 %blend.7 = (f32[64,14336]{1,0:T(8,128)}, bf16[1,64,14336]{2,1,0:T(8,128)(2,1)}) custom-call(bf16[1,64,14336]{2,1,0:T(8,128)(2,1)S(1)} %copy-done, f32[8,128]{1,0:T(8,128)S(1)} %broadcast_in_dim.3.share, bf16[64,1920]{1,0:T(8,128)(2,1)S(1)} %collective-permute-done.16.refs_0_, ...), custom_call_target="tpu_custom_call", output_to_operand_aliasing={{0}: (3, {}), {1}: (4, {})} | custom-call | flops 1 | bytes 1 | tf_op jit(solution)/shard_map/blend/pallas_call | solution.py:279
  (26 shorter events, 0.5 us)
Async XLA Ops:
  2.3 2.9 %collective-permute-start = (bf16[64,2048]{1,0:T(8,128)(2,1)S(1)}, bf16[64,2048]{1,0:T(8,128)(2,1)S(1)}, u32[]{:S(2)}, u32[]{:S(2)}) collective-permute-start(bf16[64,2048]{1,0:T(8,128)(2,1)S(1)} %codes.3.refs_0_), channel_id=1, source_target_pairs={{0,64},{64,0},{128,192},{192,128},{1,65},{65,1},{129,193},{193,129... | collective-permute-start | bytes 786440 | tf_op jit(solution)/shard_map/ppermute | solution.py:287
  5.1 10.4 %copy-start.1 = (s32[64,28]{0,1:T(8,128)S(1)}, s32[64,28]{0,1:T(8,128)}, u32[]{:S(2)}) copy-start(s32[64,28]{0,1:T(8,128)} %param.10) | copy-start | bytes 21508
  5.1 8.9 %collective-permute-start.5 = (bf16[64,1536]{1,0:T(8,128)(2,1)S(1)}, bf16[64,1536]{1,0:T(8,128)(2,1)S(1)}, u32[]{:S(2)}, u32[]{:S(2)}) collective-permute-start(bf16[64,1536]{1,0:T(8,128)(2,1)S(1)} %get-tuple-element.45), channel_id=1, source_target_pairs={{0,64},{64,0},{128,192},{192,128},{1,65},{65,1},{129,193},{193,129... | collective-permute-start | bytes 589832 | tf_op jit(solution)/shard_map/ppermute | solution.py:287
  5.3 18.7 %collective-permute-start.4 = (bf16[64,2048]{1,0:T(8,128)(2,1)S(1)}, bf16[64,2048]{1,0:T(8,128)(2,1)S(1)}, u32[]{:S(2)}, u32[]{:S(2)}) collective-permute-start(bf16[64,2048]{1,0:T(8,128)(2,1)S(1)} %pair.2.refs_0_), channel_id=1, source_target_pairs={{0,128},{128,0},{64,192},{192,64},{1,129},{129,1},{65,193},{193,65... | collective-permute-start | bytes 786440 | tf_op jit(solution)/shard_map/ppermute | solution.py:290
  14.0 20.2 %collective-permute-start.6 = (bf16[64,1536]{1,0:T(8,128)(2,1)S(1)}, bf16[64,1536]{1,0:T(8,128)(2,1)S(1)}, u32[]{:S(2)}, u32[]{:S(2)}) collective-permute-start(bf16[64,1536]{1,0:T(8,128)(2,1)S(1)} %pair.3), channel_id=1, source_target_pairs={{0,128},{128,0},{64,192},{192,64},{1,129},{129,1},{65,193},{193,65... | collective-permute-start | bytes 589832 | tf_op jit(solution)/shard_map/ppermute | solution.py:290
  14.1 2.4 %collective-permute-start.1 = (bf16[64,1280]{1,0:T(8,128)(2,1)S(1)}, bf16[64,1280]{1,0:T(8,128)(2,1)S(1)}, u32[]{:S(2)}, u32[]{:S(2)}) collective-permute-start(bf16[64,1280]{1,0:T(8,128)(2,1)S(1)} %get-tuple-element.36), channel_id=1, source_target_pairs={{0,64},{64,0},{128,192},{192,128},{1,65},{65,1},{129,193},{193,129... | collective-permute-start | bytes 491528 | tf_op jit(solution)/shard_map/ppermute | solution.py:287
  15.0 1.4 %collective-permute-start.2 = (bf16[64,1152]{1,0:T(8,128)(2,1)S(1)}, bf16[64,1152]{1,0:T(8,128)(2,1)S(1)}, u32[]{:S(2)}, u32[]{:S(2)}) collective-permute-start(bf16[64,1152]{1,0:T(8,128)(2,1)S(1)} %get-tuple-element.37), channel_id=1, source_target_pairs={{0,64},{64,0},{128,192},{192,128},{1,65},{65,1},{129,193},{193,129... | collective-permute-start | bytes 442376 | tf_op jit(solution)/shard_map/ppermute | solution.py:287
  15.1 1.5 %collective-permute-start.3 = (bf16[64,1152]{1,0:T(8,128)(2,1)S(1)}, bf16[64,1152]{1,0:T(8,128)(2,1)S(1)}, u32[]{:S(2)}, u32[]{:S(2)}) collective-permute-start(bf16[64,1152]{1,0:T(8,128)(2,1)S(1)} %get-tuple-element.38), channel_id=1, source_target_pairs={{0,64},{64,0},{128,192},{192,128},{1,65},{65,1},{129,193},{193,129... | collective-permute-start | bytes 442376 | tf_op jit(solution)/shard_map/ppermute | solution.py:287
  18.5 27.4 %copy-start.2 = (s32[2]{0:T(128)S(1)}, s32[2]{0:T(128)}, u32[]{:S(2)}) copy-start(s32[2]{0:T(128)} %param.11) | copy-start | bytes 28
  18.5 29.3 %copy-start = (bf16[1,64,14336]{2,1,0:T(8,128)(2,1)S(1)}, bf16[1,64,14336]{2,1,0:T(8,128)(2,1)}, u32[]{:S(2)}) copy-start(bf16[1,64,14336]{2,1,0:T(8,128)(2,1)} %local.15) | copy-start | bytes 5505028
  24.3 20.8 %collective-permute-start.8 = (bf16[64,1664]{1,0:T(8,128)(2,1)S(1)}, bf16[64,1664]{1,0:T(8,128)(2,1)S(1)}, u32[]{:S(2)}, u32[]{:S(2)}) collective-permute-start(bf16[64,1664]{1,0:T(8,128)(2,1)S(1)} %get-tuple-element.47), channel_id=1, source_target_pairs={{0,128},{128,0},{64,192},{192,64},{1,129},{129,1},{65,193},{193,65... | collective-permute-start | bytes 638984 | tf_op jit(solution)/shard_map/ppermute | solution.py:290
  34.6 10.1 %collective-permute-start.13 = (f32[64,640]{1,0:T(8,128)S(1)}, f32[64,640]{1,0:T(8,128)S(1)}, u32[]{:S(2)}, u32[]{:S(2)}) collective-permute-start(f32[64,640]{1,0:T(8,128)S(1)} %get-tuple-element.50.refs_2_), channel_id=1, source_target_pairs={{0,64},{64,0},{128,192},{192,128},{1,65},{65,1},{129,193},{193,129... | collective-permute-start | bytes 491528 | tf_op jit(solution)/shard_map/ppermute | solution.py:287
  38.5 6.7 %collective-permute-start.14 = (f32[64,640]{1,0:T(8,128)S(1)}, f32[64,640]{1,0:T(8,128)S(1)}, u32[]{:S(2)}, u32[]{:S(2)}) collective-permute-start(f32[64,640]{1,0:T(8,128)S(1)} %get-tuple-element.51.refs_3_), channel_id=1, source_target_pairs={{0,64},{64,0},{128,192},{192,128},{1,65},{65,1},{129,193},{193,129... | collective-permute-start | bytes 491528 | tf_op jit(solution)/shard_map/ppermute | solution.py:287
  38.6 7.1 %collective-permute-start.15 = (f32[64,640]{1,0:T(8,128)S(1)}, f32[64,640]{1,0:T(8,128)S(1)}, u32[]{:S(2)}, u32[]{:S(2)}) collective-permute-start(f32[64,640]{1,0:T(8,128)S(1)} %get-tuple-element.52.refs_4_), channel_id=1, source_target_pairs={{0,64},{64,0},{128,192},{192,128},{1,65},{65,1},{129,193},{193,129... | collective-permute-start | bytes 491528 | tf_op jit(solution)/shard_map/ppermute | solution.py:287
  39.0 15.2 %collective-permute-start.7 = (bf16[64,1920]{1,0:T(8,128)(2,1)S(1)}, bf16[64,1920]{1,0:T(8,128)(2,1)S(1)}, u32[]{:S(2)}, u32[]{:S(2)}) collective-permute-start(bf16[64,1920]{1,0:T(8,128)(2,1)S(1)} %get-tuple-element.46), channel_id=1, source_target_pairs={{0,128},{128,0},{64,192},{192,64},{1,129},{129,1},{65,193},{193,65... | collective-permute-start | bytes 737288 | tf_op jit(solution)/shard_map/ppermute | solution.py:290
  44.7 3.2 %collective-permute-start.11 = (f32[64,896]{1,0:T(8,128)S(1)}, f32[64,896]{1,0:T(8,128)S(1)}, u32[]{:S(2)}, u32[]{:S(2)}) collective-permute-start(f32[64,896]{1,0:T(8,128)S(1)} %get-tuple-element.48.refs_0_), channel_id=1, source_target_pairs={{0,64},{64,0},{128,192},{192,128},{1,65},{65,1},{129,193},{193,129... | collective-permute-start | bytes 688136 | tf_op jit(solution)/shard_map/ppermute | solution.py:287
  45.0 2.8 %collective-permute-start.12 = (f32[64,768]{1,0:T(8,128)S(1)}, f32[64,768]{1,0:T(8,128)S(1)}, u32[]{:S(2)}, u32[]{:S(2)}) collective-permute-start(f32[64,768]{1,0:T(8,128)S(1)} %get-tuple-element.49.refs_1_), channel_id=1, source_target_pairs={{0,64},{64,0},{128,192},{192,128},{1,65},{65,1},{129,193},{193,129... | collective-permute-start | bytes 589832 | tf_op jit(solution)/shard_map/ppermute | solution.py:287
  45.2 4.7 %collective-permute-start.9 = (bf16[64,896]{1,0:T(8,128)(2,1)S(1)}, bf16[64,896]{1,0:T(8,128)(2,1)S(1)}, u32[]{:S(2)}, u32[]{:S(2)}) collective-permute-start(bf16[64,896]{1,0:T(8,128)(2,1)S(1)} %slice.16), channel_id=1, source_target_pairs={{0,64},{64,0},{128,192},{192,128},{1,65},{65,1},{129,193},{193,129... | collective-permute-start | bytes 344072 | tf_op jit(solution)/shard_map/ppermute | solution.py:287
  45.7 4.2 %collective-permute-start.10 = (bf16[64,768]{1,0:T(8,128)(2,1)S(1)}, bf16[64,768]{1,0:T(8,128)(2,1)S(1)}, u32[]{:S(2)}, u32[]{:S(2)}) collective-permute-start(bf16[64,768]{1,0:T(8,128)(2,1)S(1)} %slice.17), channel_id=1, source_target_pairs={{0,64},{64,0},{128,192},{192,128},{1,65},{65,1},{129,193},{193,129... | collective-permute-start | bytes 294920 | tf_op jit(solution)/shard_map/ppermute | solution.py:287
  54.2 1.6 %collective-permute-start.16 = (bf16[64,1920]{1,0:T(8,128)(2,1)S(1)}, bf16[64,1920]{1,0:T(8,128)(2,1)S(1)}, u32[]{:S(2)}, u32[]{:S(2)}) collective-permute-start(bf16[64,1920]{1,0:T(8,128)(2,1)S(1)} %collective-permute-done.7.refs_0_), channel_id=1, source_target_pairs={{0,64},{64,0},{128,192},{192,128},{1,65},{65,1},{129,193},{193,129... | collective-permute-start | bytes 737288 | tf_op jit(solution)/shard_map/ppermute | solution.py:287

commit v3 on v2

--- a/solution.py
+++ b/solution.py
@@ -9,13 +9,13 @@
 
 BLOCK = 128
 QUARTER = 28
-FIRST, SECOND = 16, 12
-BACK_FIRST, BACK_SECOND = 13, 15
-AWAY_SECOND = (12,)
+FIRST, SECOND = 18, 10
+BACK_FIRST, BACK_SECOND = 14, 14
+AWAY_SECOND = (10,)
 CODES = (10, 9, 9)
-NEAR_FIRST, NEAR_SECOND = (7, 6), (5, 5, 5)
-FORWARD_FIRST = (7, 6)
-PIECE = 7
+NEAR_FIRST, NEAR_SECOND = (7, 7), (5, 5, 4)
+FORWARD_FIRST = (7, 7)
+PIECE = 9
 VMEM_LIMIT = 12 * 1024 * 1024
 
 momentum_decay = 0.9

time: 56.9 us -> 54.5 us (0.958)
  starting transfers between devices: 25.2 us -> 24.2 us
  waiting for transfers between devices: 14.6 us -> 13.6 us
    ppermute x13, starting transfers between devices: 8.23 us -> 7.11 us  [to_core(): return lax.ppermute(x, 'rep', [(0, 1), (1, 0), (2, 3), (3, 2)])]
    ppermute x4, waiting for transfers between devices: 13.4 us -> 12.6 us  [to_chip(): return lax.ppermute(x, 'rep', [(0, 2), (2, 0), (1, 3), (3, 1)])]
where the time goes in v3:
time: 54.5 us; the launch traced here: 54.3 us
  starting transfers between devices  24.2 us (44%)
  waiting for transfers between devices  13.6 us (25%)
  Pallas kernels  13.5 us (25%)
  between operations  2.17 us (4%)
  local copies, waits for them, and re-layouts  0.72 us (1%)
    ppermute x4, starting transfers between devices, to_chip(): return lax.ppermute(x, 'rep', [(0, 2), (2, 0), (1, 3), (3, 1)])  17.1 us
    ppermute x4, waiting for transfers between devices, to_chip(): return lax.ppermute(x, 'rep', [(0, 2), (2, 0), (1, 3), (3, 1)])  12.6 us
    ppermute x13, starting transfers between devices, to_core(): return lax.ppermute(x, 'rep', [(0, 1), (1, 0), (2, 3), (3, 2)])  7.11 us
    pallas_call x3, Pallas kernels, codes(): call(functools.partial(codes_kernel, parts, len(after)), [IN_HBM] * 3 + [...  5.8 us
    pallas_call x4, Pallas kernels, blend(): call(functools.partial(blend_kernel, parts, len(values), len(moved), len(...  5.01 us
    pallas_call x1, Pallas kernels, prepare(): call(functools.partial(prepare_kernel, len(others)), [IN_HBM] * 4 + [IN_V...  1.93 us
  transfers between devices with their start and end apart: 17, of which 6 were waited for; matrix products, arithmetic and copies ran while one was open for 1% of the time, Pallas kernels for 20%

profile of v3, /device:TPU:35, one launch (start us, length us, event | category | flops | bytes accessed | tf_op | source)
XLA Modules:
  0.0 54.3 jit_solution(9304809182228174120)
XLA Ops:
  0.6 1.6 %codes.3.refs_0_ = bf16[64,2304]{1,0:T(8,128)(2,1)S(1)} custom-call(f32[64,14336]{1,0:T(8,128)} %base.7, bf16[1,64,14336]{2,1,0:T(8,128)(2,1)} %local.15, s32[1,64,112]{2,1,0:T(8,128)} %drift.7), custom_call_target="tpu_custom_call" | custom-call | flops 1 | bytes 1 | tf_op jit(solution)/shard_map/codes/pallas_call | solution.py:239
  2.2 0.8 %collective-permute-start = (bf16[64,2304]{1,0:T(8,128)(2,1)S(1)}, bf16[64,2304]{1,0:T(8,128)(2,1)S(1)}, u32[]{:S(2)}, u32[]{:S(2)}) collective-permute-start(bf16[64,2304]{1,0:T(8,128)(2,1)S(1)} %codes.3.refs_0_), channel_id=1, source_target_pairs={{0,64},{64,0},{128,192},{192,128},{1,65},{65,1},{129,193},{193,129... | collective-permute-start | bytes 884744 | tf_op jit(solution)/shard_map/ppermute | solution.py:287
  2.9 1.9 %codes.4 = (bf16[64,2304]{1,0:T(8,128)(2,1)S(1)}, bf16[64,1280]{1,0:T(8,128)(2,1)S(1)}) custom-call(f32[64,14336]{1,0:T(8,128)} %base.7, bf16[1,64,14336]{2,1,0:T(8,128)(2,1)} %local.15, s32[1,64,112]{2,1,0:T(8,128)} %drift.7, bf16[64,2304]{1,0:T(8,128)(2,1)S(1)} %codes.3.refs_0_), custom_call_target="tpu_custom_call" | custom-call | flops 1 | bytes 1 | tf_op jit(solution)/shard_map/codes/pallas_call | solution.py:239
  5.0 6.1 %collective-permute-start.4 = (bf16[64,2304]{1,0:T(8,128)(2,1)S(1)}, bf16[64,2304]{1,0:T(8,128)(2,1)S(1)}, u32[]{:S(2)}, u32[]{:S(2)}) collective-permute-start(bf16[64,2304]{1,0:T(8,128)(2,1)S(1)} %pair.2.refs_0_), channel_id=1, source_target_pairs={{0,128},{128,0},{64,192},{192,64},{1,129},{129,1},{65,193},{193,65... | collective-permute-start | bytes 884744 | tf_op jit(solution)/shard_map/ppermute | solution.py:290
  11.1 0.3 collective-permute-start.5
  11.4 2.3 %codes.5 = (bf16[64,1280]{1,0:T(8,128)(2,1)S(1)}, bf16[64,1280]{1,0:T(8,128)(2,1)S(1)}, bf16[64,1152]{1,0:T(8,128)(2,1)S(1)}, bf16[64,1152]{1,0:T(8,128)(2,1)S(1)}) custom-call(f32[64,14336]{1,0:T(8,128)} %base.7, bf16[1,64,14336]{2,1,0:T(8,128)(2,1)} %local.15, s32[1,64,112]{2,1,0:T(8,128)} %drift.7, bf16[64,2304]{1,0:T(8,128)(2,1)S(1)} %pair.2.refs_0_), custom_call_target="tpu_custom_call" | custom-call | flops 1 | bytes 1 | tf_op jit(solution)/shard_map/codes/pallas_call | solution.py:239
  13.7 0.3 collective-permute-start.1
  14.0 0.3 collective-permute-start.2
  14.3 0.2 collective-permute-start.3
  14.6 0.2 collective-permute-start.6
  14.9 0.5 collective-permute-done.2.refs_1_
  15.4 0.3 collective-permute-done.3.refs_2_
  15.7 1.9 %prepare.1 = (f32[64,3584]{1,0:T(8,128)S(1)}, f32[64,3584]{1,0:T(8,128)S(1)}, bf16[64,3584]{1,0:T(8,128)(2,1)S(1)}, f32[64,128]{1,0:T(8,128)S(1)}, f32[64,128]{1,0:T(8,128)S(1)}) custom-call(f32[64,14336]{1,0:T(8,128)} %base.7, bf16[1,64,14336]{2,1,0:T(8,128)(2,1)} %local.15, s32[1,64,112]{2,1,0:T(8,128)} %drift.7, f32[64,3584]{1,0:T(8,128)} %momentum.1, ...), custom_call_target="tpu_custom_call" | custom-call | flops 1 | bytes 1 | tf_op jit(solution)/shard_map/prepare/pallas_call | solution.py:254
  17.7 7.2 %collective-permute-done.4.refs_0_ = bf16[64,2304]{1,0:T(8,128)(2,1)S(1)} collective-permute-done((bf16[64,2304]{1,0:T(8,128)(2,1)S(1)}, bf16[64,2304]{1,0:T(8,128)(2,1)S(1)}, u32[]{:S(2)}, u32[]{:S(2)}) %collective-permute-start.4) | collective-permute-done | bytes 294944 | tf_op jit(solution)/shard_map/ppermute | solution.py:290
  24.8 0.3 update.3
  25.2 5.2 %collective-permute-start.8 = (bf16[64,1792]{1,0:T(8,128)(2,1)S(1)}, bf16[64,1792]{1,0:T(8,128)(2,1)S(1)}, u32[]{:S(2)}, u32[]{:S(2)}) collective-permute-start(bf16[64,1792]{1,0:T(8,128)(2,1)S(1)} %get-tuple-element.47), channel_id=1, source_target_pairs={{0,128},{128,0},{64,192},{192,64},{1,129},{129,1},{65,193},{193,65... | collective-permute-start | bytes 688136 | tf_op jit(solution)/shard_map/ppermute | solution.py:290
  30.4 4.0 %collective-permute-done.6.refs_1_ = bf16[64,1280]{1,0:T(8,128)(2,1)S(1)} collective-permute-done((bf16[64,1280]{1,0:T(8,128)(2,1)S(1)}, bf16[64,1280]{1,0:T(8,128)(2,1)S(1)}, u32[]{:S(2)}, u32[]{:S(2)}) %collective-permute-start.6) | collective-permute-done | bytes 163872 | tf_op jit(solution)/shard_map/ppermute | solution.py:290
  34.4 0.3 update.2
  34.7 0.9 %collective-permute-start.15 = (f32[64,512]{1,0:T(8,128)S(1)}, f32[64,512]{1,0:T(8,128)S(1)}, u32[]{:S(2)}, u32[]{:S(2)}) collective-permute-start(f32[64,512]{1,0:T(8,128)S(1)} %get-tuple-element.52.refs_4_), channel_id=1, source_target_pairs={{0,64},{64,0},{128,192},{192,128},{1,65},{65,1},{129,193},{193,129... | collective-permute-start | bytes 393224 | tf_op jit(solution)/shard_map/ppermute | solution.py:287
  35.7 0.4 collective-permute-start.14
  36.1 5.6 %collective-permute-start.7 = (bf16[64,1792]{1,0:T(8,128)(2,1)S(1)}, bf16[64,1792]{1,0:T(8,128)(2,1)S(1)}, u32[]{:S(2)}, u32[]{:S(2)}) collective-permute-start(bf16[64,1792]{1,0:T(8,128)(2,1)S(1)} %get-tuple-element.46), channel_id=1, source_target_pairs={{0,128},{128,0},{64,192},{192,64},{1,129},{129,1},{65,193},{193,65... | collective-permute-start | bytes 688136 | tf_op jit(solution)/shard_map/ppermute | solution.py:290
  41.7 0.4 collective-permute-start.11
  42.1 1.5 %collective-permute-done.8.refs_0_ = bf16[64,1792]{1,0:T(8,128)(2,1)S(1)} collective-permute-done((bf16[64,1792]{1,0:T(8,128)(2,1)S(1)}, bf16[64,1792]{1,0:T(8,128)(2,1)S(1)}, u32[]{:S(2)}, u32[]{:S(2)}) %collective-permute-start.8) | collective-permute-done | bytes 229408 | tf_op jit(solution)/shard_map/ppermute | solution.py:290
  43.5 2.1 %collective-permute-start.12 = (f32[64,896]{1,0:T(8,128)S(1)}, f32[64,896]{1,0:T(8,128)S(1)}, u32[]{:S(2)}, u32[]{:S(2)}) collective-permute-start(f32[64,896]{1,0:T(8,128)S(1)} %get-tuple-element.49.refs_1_), channel_id=1, source_target_pairs={{0,64},{64,0},{128,192},{192,128},{1,65},{65,1},{129,193},{193,129... | collective-permute-start | bytes 688136 | tf_op jit(solution)/shard_map/ppermute | solution.py:287
  45.7 0.5 collective-permute-start.9
  46.2 0.6 %fusion.1 = (s32[1]{0:T(128)}, s32[1]{0:T(128)}) fusion(s32[2]{0:T(128)S(1)} %copy-done.2), kind=kLoop, calls=%fused_computation.1 | loop fusion | bytes 16 | tf_op jit(solution)/shard_map/slice | solution.py:207
  48.2 2.0 %blend.4 = (f32[64,14336]{1,0:T(8,128)}, bf16[1,64,14336]{2,1,0:T(8,128)(2,1)}, f32[64,3584]{1,0:T(8,128)}) custom-call(bf16[1,64,14336]{2,1,0:T(8,128)(2,1)S(1)} %copy-done, f32[8,128]{1,0:T(8,128)S(1)} %broadcast_in_dim.3.share, f32[64,896]{1,0:T(8,128)S(1)} %get-tuple-element.48.refs_0_, f32[64,896]{1,0:T(8,128)S(1)} %get-tuple-element.49.refs_1_, ...), custom_call_target="tpu_custom_call" | custom-call | flops 1 | bytes 1 | tf_op jit(solution)/shard_map/blend/pallas_call | solution.py:279
  50.2 1.2 %blend.5 = (f32[64,14336]{1,0:T(8,128)}, bf16[1,64,14336]{2,1,0:T(8,128)(2,1)}) custom-call(bf16[1,64,14336]{2,1,0:T(8,128)(2,1)S(1)} %copy-done, f32[8,128]{1,0:T(8,128)S(1)} %broadcast_in_dim.3.share, bf16[64,1792]{1,0:T(8,128)(2,1)S(1)} %collective-permute-done.8.refs_0_, ...), custom_call_target="tpu_custom_call", output_to_operand_aliasing={{0}: (5, {}), {1}: (6, {})} | custom-call | flops 1 | bytes 1 | tf_op jit(solution)/shard_map/blend/pallas_call | solution.py:279
  51.4 0.8 %collective-permute-start.16 = (bf16[64,1792]{1,0:T(8,128)(2,1)S(1)}, bf16[64,1792]{1,0:T(8,128)(2,1)S(1)}, u32[]{:S(2)}, u32[]{:S(2)}) collective-permute-start(bf16[64,1792]{1,0:T(8,128)(2,1)S(1)} %collective-permute-done.7.refs_0_), channel_id=1, source_target_pairs={{0,64},{64,0},{128,192},{192,128},{1,65},{65,1},{129,193},{193,129... | collective-permute-start | bytes 688136 | tf_op jit(solution)/shard_map/ppermute | solution.py:287
  52.2 0.9 %blend.6 = (f32[64,14336]{1,0:T(8,128)}, bf16[1,64,14336]{2,1,0:T(8,128)(2,1)}) custom-call(bf16[1,64,14336]{2,1,0:T(8,128)(2,1)S(1)} %copy-done, f32[8,128]{1,0:T(8,128)S(1)} %broadcast_in_dim.3.share, bf16[64,1792]{1,0:T(8,128)(2,1)S(1)} %collective-permute-done.7.refs_0_, ...), custom_call_target="tpu_custom_call", output_to_operand_aliasing={{0}: (3, {}), {1}: (4, {})} | custom-call | flops 1 | bytes 1 | tf_op jit(solution)/shard_map/blend/pallas_call | solution.py:279
  53.2 0.2 collective-permute-done.16.refs_0_
  53.4 0.9 %blend.7 = (f32[64,14336]{1,0:T(8,128)}, bf16[1,64,14336]{2,1,0:T(8,128)(2,1)}) custom-call(bf16[1,64,14336]{2,1,0:T(8,128)(2,1)S(1)} %copy-done, f32[8,128]{1,0:T(8,128)S(1)} %broadcast_in_dim.3.share, bf16[64,1792]{1,0:T(8,128)(2,1)S(1)} %collective-permute-done.16.refs_0_, ...), custom_call_target="tpu_custom_call", output_to_operand_aliasing={{0}: (3, {}), {1}: (4, {})} | custom-call | flops 1 | bytes 1 | tf_op jit(solution)/shard_map/blend/pallas_call | solution.py:279
  (25 shorter events, 0.5 us)
Async XLA Ops:
  2.2 2.7 %collective-permute-start = (bf16[64,2304]{1,0:T(8,128)(2,1)S(1)}, bf16[64,2304]{1,0:T(8,128)(2,1)S(1)}, u32[]{:S(2)}, u32[]{:S(2)}) collective-permute-start(bf16[64,2304]{1,0:T(8,128)(2,1)S(1)} %codes.3.refs_0_), channel_id=1, source_target_pairs={{0,64},{64,0},{128,192},{192,128},{1,65},{65,1},{129,193},{193,129... | collective-permute-start | bytes 884744 | tf_op jit(solution)/shard_map/ppermute | solution.py:287
  4.9 9.9 %copy-start.1 = (s32[64,28]{0,1:T(8,128)S(1)}, s32[64,28]{0,1:T(8,128)}, u32[]{:S(2)}) copy-start(s32[64,28]{0,1:T(8,128)} %param.10) | copy-start | bytes 21508
  5.0 19.8 %collective-permute-start.4 = (bf16[64,2304]{1,0:T(8,128)(2,1)S(1)}, bf16[64,2304]{1,0:T(8,128)(2,1)S(1)}, u32[]{:S(2)}, u32[]{:S(2)}) collective-permute-start(bf16[64,2304]{1,0:T(8,128)(2,1)S(1)} %pair.2.refs_0_), channel_id=1, source_target_pairs={{0,128},{128,0},{64,192},{192,64},{1,129},{129,1},{65,193},{193,65... | collective-permute-start | bytes 884744 | tf_op jit(solution)/shard_map/ppermute | solution.py:290
  11.1 3.4 %collective-permute-start.5 = (bf16[64,1280]{1,0:T(8,128)(2,1)S(1)}, bf16[64,1280]{1,0:T(8,128)(2,1)S(1)}, u32[]{:S(2)}, u32[]{:S(2)}) collective-permute-start(bf16[64,1280]{1,0:T(8,128)(2,1)S(1)} %get-tuple-element.45), channel_id=1, source_target_pairs={{0,64},{64,0},{128,192},{192,128},{1,65},{65,1},{129,193},{193,129... | collective-permute-start | bytes 491528 | tf_op jit(solution)/shard_map/ppermute | solution.py:287
  13.7 2.0 %collective-permute-start.1 = (bf16[64,1280]{1,0:T(8,128)(2,1)S(1)}, bf16[64,1280]{1,0:T(8,128)(2,1)S(1)}, u32[]{:S(2)}, u32[]{:S(2)}) collective-permute-start(bf16[64,1280]{1,0:T(8,128)(2,1)S(1)} %get-tuple-element.36), channel_id=1, source_target_pairs={{0,64},{64,0},{128,192},{192,128},{1,65},{65,1},{129,193},{193,129... | collective-permute-start | bytes 491528 | tf_op jit(solution)/shard_map/ppermute | solution.py:287
  14.0 1.4 %collective-permute-start.2 = (bf16[64,1152]{1,0:T(8,128)(2,1)S(1)}, bf16[64,1152]{1,0:T(8,128)(2,1)S(1)}, u32[]{:S(2)}, u32[]{:S(2)}) collective-permute-start(bf16[64,1152]{1,0:T(8,128)(2,1)S(1)} %get-tuple-element.37), channel_id=1, source_target_pairs={{0,64},{64,0},{128,192},{192,128},{1,65},{65,1},{129,193},{193,129... | collective-permute-start | bytes 442376 | tf_op jit(solution)/shard_map/ppermute | solution.py:287
  14.3 1.4 %collective-permute-start.3 = (bf16[64,1152]{1,0:T(8,128)(2,1)S(1)}, bf16[64,1152]{1,0:T(8,128)(2,1)S(1)}, u32[]{:S(2)}, u32[]{:S(2)}) collective-permute-start(bf16[64,1152]{1,0:T(8,128)(2,1)S(1)} %get-tuple-element.38), channel_id=1, source_target_pairs={{0,64},{64,0},{128,192},{192,128},{1,65},{65,1},{129,193},{193,129... | collective-permute-start | bytes 442376 | tf_op jit(solution)/shard_map/ppermute | solution.py:287
  14.6 19.8 %collective-permute-start.6 = (bf16[64,1280]{1,0:T(8,128)(2,1)S(1)}, bf16[64,1280]{1,0:T(8,128)(2,1)S(1)}, u32[]{:S(2)}, u32[]{:S(2)}) collective-permute-start(bf16[64,1280]{1,0:T(8,128)(2,1)S(1)} %pair.3), channel_id=1, source_target_pairs={{0,128},{128,0},{64,192},{192,64},{1,129},{129,1},{65,193},{193,65... | collective-permute-start | bytes 491528 | tf_op jit(solution)/shard_map/ppermute | solution.py:290
  17.6 28.6 %copy-start.2 = (s32[2]{0:T(128)S(1)}, s32[2]{0:T(128)}, u32[]{:S(2)}) copy-start(s32[2]{0:T(128)} %param.11) | copy-start | bytes 28
  17.6 30.6 %copy-start = (bf16[1,64,14336]{2,1,0:T(8,128)(2,1)S(1)}, bf16[1,64,14336]{2,1,0:T(8,128)(2,1)}, u32[]{:S(2)}) copy-start(bf16[1,64,14336]{2,1,0:T(8,128)(2,1)} %local.15) | copy-start | bytes 5505028
  25.2 18.4 %collective-permute-start.8 = (bf16[64,1792]{1,0:T(8,128)(2,1)S(1)}, bf16[64,1792]{1,0:T(8,128)(2,1)S(1)}, u32[]{:S(2)}, u32[]{:S(2)}) collective-permute-start(bf16[64,1792]{1,0:T(8,128)(2,1)S(1)} %get-tuple-element.47), channel_id=1, source_target_pairs={{0,128},{128,0},{64,192},{192,64},{1,129},{129,1},{65,193},{193,65... | collective-permute-start | bytes 688136 | tf_op jit(solution)/shard_map/ppermute | solution.py:290
  34.7 7.0 %collective-permute-start.15 = (f32[64,512]{1,0:T(8,128)S(1)}, f32[64,512]{1,0:T(8,128)S(1)}, u32[]{:S(2)}, u32[]{:S(2)}) collective-permute-start(f32[64,512]{1,0:T(8,128)S(1)} %get-tuple-element.52.refs_4_), channel_id=1, source_target_pairs={{0,64},{64,0},{128,192},{192,128},{1,65},{65,1},{129,193},{193,129... | collective-permute-start | bytes 393224 | tf_op jit(solution)/shard_map/ppermute | solution.py:287
  35.6 10.0 %collective-permute-start.13 = (f32[64,640]{1,0:T(8,128)S(1)}, f32[64,640]{1,0:T(8,128)S(1)}, u32[]{:S(2)}, u32[]{:S(2)}) collective-permute-start(f32[64,640]{1,0:T(8,128)S(1)} %get-tuple-element.50.refs_2_), channel_id=1, source_target_pairs={{0,64},{64,0},{128,192},{192,128},{1,65},{65,1},{129,193},{193,129... | collective-permute-start | bytes 491528 | tf_op jit(solution)/shard_map/ppermute | solution.py:287
  35.7 10.0 %collective-permute-start.14 = (f32[64,640]{1,0:T(8,128)S(1)}, f32[64,640]{1,0:T(8,128)S(1)}, u32[]{:S(2)}, u32[]{:S(2)}) collective-permute-start(f32[64,640]{1,0:T(8,128)S(1)} %get-tuple-element.51.refs_3_), channel_id=1, source_target_pairs={{0,64},{64,0},{128,192},{192,128},{1,65},{65,1},{129,193},{193,129... | collective-permute-start | bytes 491528 | tf_op jit(solution)/shard_map/ppermute | solution.py:287
  36.1 15.3 %collective-permute-start.7 = (bf16[64,1792]{1,0:T(8,128)(2,1)S(1)}, bf16[64,1792]{1,0:T(8,128)(2,1)S(1)}, u32[]{:S(2)}, u32[]{:S(2)}) collective-permute-start(bf16[64,1792]{1,0:T(8,128)(2,1)S(1)} %get-tuple-element.46), channel_id=1, source_target_pairs={{0,128},{128,0},{64,192},{192,64},{1,129},{129,1},{65,193},{193,65... | collective-permute-start | bytes 688136 | tf_op jit(solution)/shard_map/ppermute | solution.py:290
  41.7 6.4 %collective-permute-start.11 = (f32[64,896]{1,0:T(8,128)S(1)}, f32[64,896]{1,0:T(8,128)S(1)}, u32[]{:S(2)}, u32[]{:S(2)}) collective-permute-start(f32[64,896]{1,0:T(8,128)S(1)} %get-tuple-element.48.refs_0_), channel_id=1, source_target_pairs={{0,64},{64,0},{128,192},{192,128},{1,65},{65,1},{129,193},{193,129... | collective-permute-start | bytes 688136 | tf_op jit(solution)/shard_map/ppermute | solution.py:287
  43.5 4.6 %collective-permute-start.12 = (f32[64,896]{1,0:T(8,128)S(1)}, f32[64,896]{1,0:T(8,128)S(1)}, u32[]{:S(2)}, u32[]{:S(2)}) collective-permute-start(f32[64,896]{1,0:T(8,128)S(1)} %get-tuple-element.49.refs_1_), channel_id=1, source_target_pairs={{0,64},{64,0},{128,192},{192,128},{1,65},{65,1},{129,193},{193,129... | collective-permute-start | bytes 688136 | tf_op jit(solution)/shard_map/ppermute | solution.py:287
  45.6 4.6 %collective-permute-start.10 = (bf16[64,896]{1,0:T(8,128)(2,1)S(1)}, bf16[64,896]{1,0:T(8,128)(2,1)S(1)}, u32[]{:S(2)}, u32[]{:S(2)}) collective-permute-start(bf16[64,896]{1,0:T(8,128)(2,1)S(1)} %get-tuple-element.67), channel_id=1, source_target_pairs={{0,64},{64,0},{128,192},{192,128},{1,65},{65,1},{129,193},{193,129... | collective-permute-start | bytes 344072 | tf_op jit(solution)/shard_map/ppermute | solution.py:287
  45.7 4.5 %collective-permute-start.9 = (bf16[64,896]{1,0:T(8,128)(2,1)S(1)}, bf16[64,896]{1,0:T(8,128)(2,1)S(1)}, u32[]{:S(2)}, u32[]{:S(2)}) collective-permute-start(bf16[64,896]{1,0:T(8,128)(2,1)S(1)} %get-tuple-element.68), channel_id=1, source_target_pairs={{0,64},{64,0},{128,192},{192,128},{1,65},{65,1},{129,193},{193,129... | collective-permute-start | bytes 344072 | tf_op jit(solution)/shard_map/ppermute | solution.py:287
  51.4 1.9 %collective-permute-start.16 = (bf16[64,1792]{1,0:T(8,128)(2,1)S(1)}, bf16[64,1792]{1,0:T(8,128)(2,1)S(1)}, u32[]{:S(2)}, u32[]{:S(2)}) collective-permute-start(bf16[64,1792]{1,0:T(8,128)(2,1)S(1)} %collective-permute-done.7.refs_0_), channel_id=1, source_target_pairs={{0,64},{64,0},{128,192},{192,128},{1,65},{65,1},{129,193},{193,129... | collective-permute-start | bytes 688136 | tf_op jit(solution)/shard_map/ppermute | solution.py:287

commit v4 on v3

--- a/solution.py
+++ b/solution.py
@@ -12,8 +12,8 @@
 FIRST, SECOND = 18, 10
 BACK_FIRST, BACK_SECOND = 14, 14
 AWAY_SECOND = (10,)
-CODES = (10, 9, 9)
-NEAR_FIRST, NEAR_SECOND = (7, 7), (5, 5, 4)
+CODES = (12, 8, 8)
+NEAR_FIRST, NEAR_SECOND = (8, 6), (5, 5, 4)
 FORWARD_FIRST = (7, 7)
 PIECE = 9
 VMEM_LIMIT = 12 * 1024 * 1024

time: 54.5 us -> 54.5 us (level)
  transfers between devices with their start and end apart: 17 -> 17, of which waited for: 6 -> 7; matrix products, arithmetic and copies ran while one was open for 1% -> 1% of each run, Pallas kernels for 20% -> 20%
where the time goes in v4:
time: 54.5 us; the launch traced here: 54.3 us
  starting transfers between devices  23.9 us (44%)
  waiting for transfers between devices  14 us (26%)
  Pallas kernels  13.5 us (25%)
  between operations  2.17 us (4%)
  local copies, waits for them, and re-layouts  0.72 us (1%)
    ppermute x4, starting transfers between devices, to_chip(): return lax.ppermute(x, 'rep', [(0, 2), (2, 0), (1, 3), (3, 1)])  17 us
    ppermute x4, waiting for transfers between devices, to_chip(): return lax.ppermute(x, 'rep', [(0, 2), (2, 0), (1, 3), (3, 1)])  12.6 us
    ppermute x13, starting transfers between devices, to_core(): return lax.ppermute(x, 'rep', [(0, 1), (1, 0), (2, 3), (3, 2)])  6.87 us
    pallas_call x3, Pallas kernels, codes(): call(functools.partial(codes_kernel, parts, len(after)), [IN_HBM] * 3 + [...  5.8 us
    pallas_call x4, Pallas kernels, blend(): call(functools.partial(blend_kernel, parts, len(values), len(moved), len(...  5.01 us
    pallas_call x1, Pallas kernels, prepare(): call(functools.partial(prepare_kernel, len(others)), [IN_HBM] * 4 + [IN_V...  1.93 us
    ppermute x13, waiting for transfers between devices, to_core(): return lax.ppermute(x, 'rep', [(0, 1), (1, 0), (2, 3), (3, 2)])  1.37 us
  transfers between devices with their start and end apart: 17, of which 7 were waited for; matrix products, arithmetic and copies ran while one was open for 1% of the time, Pallas kernels for 20%

profile of v4, /device:TPU:35, one launch (start us, length us, event | category | flops | bytes accessed | tf_op | source)
XLA Modules:
  0.0 54.3 jit_solution(15366406641880540858)
XLA Ops:
  0.6 1.6 %codes.3.refs_0_ = bf16[64,2304]{1,0:T(8,128)(2,1)S(1)} custom-call(f32[64,14336]{1,0:T(8,128)} %base.7, bf16[1,64,14336]{2,1,0:T(8,128)(2,1)} %local.15, s32[1,64,112]{2,1,0:T(8,128)} %drift.7), custom_call_target="tpu_custom_call" | custom-call | flops 1 | bytes 1 | tf_op jit(solution)/shard_map/codes/pallas_call | solution.py:239
  2.2 0.8 %collective-permute-start = (bf16[64,2304]{1,0:T(8,128)(2,1)S(1)}, bf16[64,2304]{1,0:T(8,128)(2,1)S(1)}, u32[]{:S(2)}, u32[]{:S(2)}) collective-permute-start(bf16[64,2304]{1,0:T(8,128)(2,1)S(1)} %codes.3.refs_0_), channel_id=1, source_target_pairs={{0,64},{64,0},{128,192},{192,128},{1,65},{65,1},{129,193},{193,129... | collective-permute-start | bytes 884744 | tf_op jit(solution)/shard_map/ppermute | solution.py:287
  2.9 1.9 %codes.4 = (bf16[64,2304]{1,0:T(8,128)(2,1)S(1)}, bf16[64,1280]{1,0:T(8,128)(2,1)S(1)}) custom-call(f32[64,14336]{1,0:T(8,128)} %base.7, bf16[1,64,14336]{2,1,0:T(8,128)(2,1)} %local.15, s32[1,64,112]{2,1,0:T(8,128)} %drift.7, bf16[64,2304]{1,0:T(8,128)(2,1)S(1)} %codes.3.refs_0_), custom_call_target="tpu_custom_call" | custom-call | flops 1 | bytes 1 | tf_op jit(solution)/shard_map/codes/pallas_call | solution.py:239
  5.0 6.1 %collective-permute-start.4 = (bf16[64,2304]{1,0:T(8,128)(2,1)S(1)}, bf16[64,2304]{1,0:T(8,128)(2,1)S(1)}, u32[]{:S(2)}, u32[]{:S(2)}) collective-permute-start(bf16[64,2304]{1,0:T(8,128)(2,1)S(1)} %pair.2.refs_0_), channel_id=1, source_target_pairs={{0,128},{128,0},{64,192},{192,64},{1,129},{129,1},{65,193},{193,65... | collective-permute-start | bytes 884744 | tf_op jit(solution)/shard_map/ppermute | solution.py:290
  11.1 0.3 collective-permute-start.5
  11.4 2.3 %codes.5 = (bf16[64,1280]{1,0:T(8,128)(2,1)S(1)}, bf16[64,1536]{1,0:T(8,128)(2,1)S(1)}, bf16[64,1024]{1,0:T(8,128)(2,1)S(1)}, bf16[64,1024]{1,0:T(8,128)(2,1)S(1)}) custom-call(f32[64,14336]{1,0:T(8,128)} %base.7, bf16[1,64,14336]{2,1,0:T(8,128)(2,1)} %local.15, s32[1,64,112]{2,1,0:T(8,128)} %drift.7, bf16[64,2304]{1,0:T(8,128)(2,1)S(1)} %pair.2.refs_0_), custom_call_target="tpu_custom_call" | custom-call | flops 1 | bytes 1 | tf_op jit(solution)/shard_map/codes/pallas_call | solution.py:239
  13.7 0.3 collective-permute-start.1
  14.0 0.3 collective-permute-start.2
  14.3 0.2 collective-permute-start.3
  14.6 0.2 collective-permute-start.6
  14.9 0.5 %collective-permute-done.2.refs_1_ = bf16[64,1024]{1,0:T(8,128)(2,1)S(1)} collective-permute-done((bf16[64,1024]{1,0:T(8,128)(2,1)S(1)}, bf16[64,1024]{1,0:T(8,128)(2,1)S(1)}, u32[]{:S(2)}, u32[]{:S(2)}) %collective-permute-start.2) | collective-permute-done | bytes 131104 | tf_op jit(solution)/shard_map/ppermute | solution.py:287
  15.4 0.2 collective-permute-done.3.refs_2_
  15.7 1.9 %prepare.1 = (f32[64,3584]{1,0:T(8,128)S(1)}, f32[64,3584]{1,0:T(8,128)S(1)}, bf16[64,3584]{1,0:T(8,128)(2,1)S(1)}, f32[64,128]{1,0:T(8,128)S(1)}, f32[64,128]{1,0:T(8,128)S(1)}) custom-call(f32[64,14336]{1,0:T(8,128)} %base.7, bf16[1,64,14336]{2,1,0:T(8,128)(2,1)} %local.15, s32[1,64,112]{2,1,0:T(8,128)} %drift.7, f32[64,3584]{1,0:T(8,128)} %momentum.1, ...), custom_call_target="tpu_custom_call" | custom-call | flops 1 | bytes 1 | tf_op jit(solution)/shard_map/prepare/pallas_call | solution.py:254
  17.6 7.2 %collective-permute-done.4.refs_0_ = bf16[64,2304]{1,0:T(8,128)(2,1)S(1)} collective-permute-done((bf16[64,2304]{1,0:T(8,128)(2,1)S(1)}, bf16[64,2304]{1,0:T(8,128)(2,1)S(1)}, u32[]{:S(2)}, u32[]{:S(2)}) %collective-permute-start.4) | collective-permute-done | bytes 294944 | tf_op jit(solution)/shard_map/ppermute | solution.py:290
  24.8 0.3 update.3
  25.2 5.2 %collective-permute-start.8 = (bf16[64,1792]{1,0:T(8,128)(2,1)S(1)}, bf16[64,1792]{1,0:T(8,128)(2,1)S(1)}, u32[]{:S(2)}, u32[]{:S(2)}) collective-permute-start(bf16[64,1792]{1,0:T(8,128)(2,1)S(1)} %get-tuple-element.47), channel_id=1, source_target_pairs={{0,128},{128,0},{64,192},{192,64},{1,129},{129,1},{65,193},{193,65... | collective-permute-start | bytes 688136 | tf_op jit(solution)/shard_map/ppermute | solution.py:290
  30.4 4.0 %collective-permute-done.6.refs_1_ = bf16[64,1280]{1,0:T(8,128)(2,1)S(1)} collective-permute-done((bf16[64,1280]{1,0:T(8,128)(2,1)S(1)}, bf16[64,1280]{1,0:T(8,128)(2,1)S(1)}, u32[]{:S(2)}, u32[]{:S(2)}) %collective-permute-start.6) | collective-permute-done | bytes 163872 | tf_op jit(solution)/shard_map/ppermute | solution.py:290
  34.4 0.3 update.2
  34.7 0.9 %collective-permute-start.15 = (f32[64,512]{1,0:T(8,128)S(1)}, f32[64,512]{1,0:T(8,128)S(1)}, u32[]{:S(2)}, u32[]{:S(2)}) collective-permute-start(f32[64,512]{1,0:T(8,128)S(1)} %get-tuple-element.52.refs_4_), channel_id=1, source_target_pairs={{0,64},{64,0},{128,192},{192,128},{1,65},{65,1},{129,193},{193,129... | collective-permute-start | bytes 393224 | tf_op jit(solution)/shard_map/ppermute | solution.py:287
  35.7 0.4 collective-permute-start.14
  36.3 0.4 collective-permute-done.15.refs_9_
  36.6 5.5 %collective-permute-start.7 = (bf16[64,1792]{1,0:T(8,128)(2,1)S(1)}, bf16[64,1792]{1,0:T(8,128)(2,1)S(1)}, u32[]{:S(2)}, u32[]{:S(2)}) collective-permute-start(bf16[64,1792]{1,0:T(8,128)(2,1)S(1)} %get-tuple-element.46), channel_id=1, source_target_pairs={{0,128},{128,0},{64,192},{192,64},{1,129},{129,1},{65,193},{193,65... | collective-permute-start | bytes 688136 | tf_op jit(solution)/shard_map/ppermute | solution.py:290
  42.1 1.4 %collective-permute-done.8.refs_0_ = bf16[64,1792]{1,0:T(8,128)(2,1)S(1)} collective-permute-done((bf16[64,1792]{1,0:T(8,128)(2,1)S(1)}, bf16[64,1792]{1,0:T(8,128)(2,1)S(1)}, u32[]{:S(2)}, u32[]{:S(2)}) %collective-permute-start.8) | collective-permute-done | bytes 229408 | tf_op jit(solution)/shard_map/ppermute | solution.py:290
  43.5 2.1 %collective-permute-start.11 = (f32[64,1024]{1,0:T(8,128)S(1)}, f32[64,1024]{1,0:T(8,128)S(1)}, u32[]{:S(2)}, u32[]{:S(2)}) collective-permute-start(f32[64,1024]{1,0:T(8,128)S(1)} %get-tuple-element.48.refs_0_), channel_id=1, source_target_pairs={{0,64},{64,0},{128,192},{192,128},{1,65},{65,1},{129,193},{193,129... | collective-permute-start | bytes 786440 | tf_op jit(solution)/shard_map/ppermute | solution.py:287
  45.7 0.5 collective-permute-start.9
  46.2 0.6 %fusion.1 = (s32[1]{0:T(128)}, s32[1]{0:T(128)}) fusion(s32[2]{0:T(128)S(1)} %copy-done.2), kind=kLoop, calls=%fused_computation.1 | loop fusion | bytes 16 | tf_op jit(solution)/shard_map/slice | solution.py:207
  48.2 2.0 %blend.4 = (f32[64,14336]{1,0:T(8,128)}, bf16[1,64,14336]{2,1,0:T(8,128)(2,1)}, f32[64,3584]{1,0:T(8,128)}) custom-call(bf16[1,64,14336]{2,1,0:T(8,128)(2,1)S(1)} %copy-done, f32[8,128]{1,0:T(8,128)S(1)} %broadcast_in_dim.3.share, f32[64,1024]{1,0:T(8,128)S(1)} %get-tuple-element.48.refs_0_, f32[64,768]{1,0:T(8,128)S(1)} %get-tuple-element.49.refs_1_, ...), custom_call_target="tpu_custom_call" | custom-call | flops 1 | bytes 1 | tf_op jit(solution)/shard_map/blend/pallas_call | solution.py:279
  50.2 1.2 %blend.5 = (f32[64,14336]{1,0:T(8,128)}, bf16[1,64,14336]{2,1,0:T(8,128)(2,1)}) custom-call(bf16[1,64,14336]{2,1,0:T(8,128)(2,1)S(1)} %copy-done, f32[8,128]{1,0:T(8,128)S(1)} %broadcast_in_dim.3.share, bf16[64,1792]{1,0:T(8,128)(2,1)S(1)} %collective-permute-done.8.refs_0_, ...), custom_call_target="tpu_custom_call", output_to_operand_aliasing={{0}: (5, {}), {1}: (6, {})} | custom-call | flops 1 | bytes 1 | tf_op jit(solution)/shard_map/blend/pallas_call | solution.py:279
  51.4 0.8 %collective-permute-start.16 = (bf16[64,1792]{1,0:T(8,128)(2,1)S(1)}, bf16[64,1792]{1,0:T(8,128)(2,1)S(1)}, u32[]{:S(2)}, u32[]{:S(2)}) collective-permute-start(bf16[64,1792]{1,0:T(8,128)(2,1)S(1)} %collective-permute-done.7.refs_0_), channel_id=1, source_target_pairs={{0,64},{64,0},{128,192},{192,128},{1,65},{65,1},{129,193},{193,129... | collective-permute-start | bytes 688136 | tf_op jit(solution)/shard_map/ppermute | solution.py:287
  52.3 0.9 %blend.6 = (f32[64,14336]{1,0:T(8,128)}, bf16[1,64,14336]{2,1,0:T(8,128)(2,1)}) custom-call(bf16[1,64,14336]{2,1,0:T(8,128)(2,1)S(1)} %copy-done, f32[8,128]{1,0:T(8,128)S(1)} %broadcast_in_dim.3.share, bf16[64,1792]{1,0:T(8,128)(2,1)S(1)} %collective-permute-done.7.refs_0_, ...), custom_call_target="tpu_custom_call", output_to_operand_aliasing={{0}: (3, {}), {1}: (4, {})} | custom-call | flops 1 | bytes 1 | tf_op jit(solution)/shard_map/blend/pallas_call | solution.py:279
  53.2 0.2 collective-permute-done.16.refs_0_
  53.4 0.9 %blend.7 = (f32[64,14336]{1,0:T(8,128)}, bf16[1,64,14336]{2,1,0:T(8,128)(2,1)}) custom-call(bf16[1,64,14336]{2,1,0:T(8,128)(2,1)S(1)} %copy-done, f32[8,128]{1,0:T(8,128)S(1)} %broadcast_in_dim.3.share, bf16[64,1792]{1,0:T(8,128)(2,1)S(1)} %collective-permute-done.16.refs_0_, ...), custom_call_target="tpu_custom_call", output_to_operand_aliasing={{0}: (3, {}), {1}: (4, {})} | custom-call | flops 1 | bytes 1 | tf_op jit(solution)/shard_map/blend/pallas_call | solution.py:279
  (25 shorter events, 0.6 us)
Async XLA Ops:
  2.2 2.7 %collective-permute-start = (bf16[64,2304]{1,0:T(8,128)(2,1)S(1)}, bf16[64,2304]{1,0:T(8,128)(2,1)S(1)}, u32[]{:S(2)}, u32[]{:S(2)}) collective-permute-start(bf16[64,2304]{1,0:T(8,128)(2,1)S(1)} %codes.3.refs_0_), channel_id=1, source_target_pairs={{0,64},{64,0},{128,192},{192,128},{1,65},{65,1},{129,193},{193,129... | collective-permute-start | bytes 884744 | tf_op jit(solution)/shard_map/ppermute | solution.py:287
  4.9 9.9 %copy-start.1 = (s32[64,28]{0,1:T(8,128)S(1)}, s32[64,28]{0,1:T(8,128)}, u32[]{:S(2)}) copy-start(s32[64,28]{0,1:T(8,128)} %param.10) | copy-start | bytes 21508
  5.0 19.8 %collective-permute-start.4 = (bf16[64,2304]{1,0:T(8,128)(2,1)S(1)}, bf16[64,2304]{1,0:T(8,128)(2,1)S(1)}, u32[]{:S(2)}, u32[]{:S(2)}) collective-permute-start(bf16[64,2304]{1,0:T(8,128)(2,1)S(1)} %pair.2.refs_0_), channel_id=1, source_target_pairs={{0,128},{128,0},{64,192},{192,64},{1,129},{129,1},{65,193},{193,65... | collective-permute-start | bytes 884744 | tf_op jit(solution)/shard_map/ppermute | solution.py:290
  11.1 3.4 %collective-permute-start.5 = (bf16[64,1280]{1,0:T(8,128)(2,1)S(1)}, bf16[64,1280]{1,0:T(8,128)(2,1)S(1)}, u32[]{:S(2)}, u32[]{:S(2)}) collective-permute-start(bf16[64,1280]{1,0:T(8,128)(2,1)S(1)} %get-tuple-element.45), channel_id=1, source_target_pairs={{0,64},{64,0},{128,192},{192,128},{1,65},{65,1},{129,193},{193,129... | collective-permute-start | bytes 491528 | tf_op jit(solution)/shard_map/ppermute | solution.py:287
  13.7 1.9 %collective-permute-start.1 = (bf16[64,1536]{1,0:T(8,128)(2,1)S(1)}, bf16[64,1536]{1,0:T(8,128)(2,1)S(1)}, u32[]{:S(2)}, u32[]{:S(2)}) collective-permute-start(bf16[64,1536]{1,0:T(8,128)(2,1)S(1)} %get-tuple-element.36), channel_id=1, source_target_pairs={{0,64},{64,0},{128,192},{192,128},{1,65},{65,1},{129,193},{193,129... | collective-permute-start | bytes 589832 | tf_op jit(solution)/shard_map/ppermute | solution.py:287
  14.0 1.4 %collective-permute-start.2 = (bf16[64,1024]{1,0:T(8,128)(2,1)S(1)}, bf16[64,1024]{1,0:T(8,128)(2,1)S(1)}, u32[]{:S(2)}, u32[]{:S(2)}) collective-permute-start(bf16[64,1024]{1,0:T(8,128)(2,1)S(1)} %get-tuple-element.37), channel_id=1, source_target_pairs={{0,64},{64,0},{128,192},{192,128},{1,65},{65,1},{129,193},{193,129... | collective-permute-start | bytes 393224 | tf_op jit(solution)/shard_map/ppermute | solution.py:287
  14.3 1.3 %collective-permute-start.3 = (bf16[64,1024]{1,0:T(8,128)(2,1)S(1)}, bf16[64,1024]{1,0:T(8,128)(2,1)S(1)}, u32[]{:S(2)}, u32[]{:S(2)}) collective-permute-start(bf16[64,1024]{1,0:T(8,128)(2,1)S(1)} %get-tuple-element.38), channel_id=1, source_target_pairs={{0,64},{64,0},{128,192},{192,128},{1,65},{65,1},{129,193},{193,129... | collective-permute-start | bytes 393224 | tf_op jit(solution)/shard_map/ppermute | solution.py:287
  14.6 19.8 %collective-permute-start.6 = (bf16[64,1280]{1,0:T(8,128)(2,1)S(1)}, bf16[64,1280]{1,0:T(8,128)(2,1)S(1)}, u32[]{:S(2)}, u32[]{:S(2)}) collective-permute-start(bf16[64,1280]{1,0:T(8,128)(2,1)S(1)} %pair.3), channel_id=1, source_target_pairs={{0,128},{128,0},{64,192},{192,64},{1,129},{129,1},{65,193},{193,65... | collective-permute-start | bytes 491528 | tf_op jit(solution)/shard_map/ppermute | solution.py:290
  17.6 28.6 %copy-start.2 = (s32[2]{0:T(128)S(1)}, s32[2]{0:T(128)}, u32[]{:S(2)}) copy-start(s32[2]{0:T(128)} %param.11) | copy-start | bytes 28
  17.6 30.6 %copy-start = (bf16[1,64,14336]{2,1,0:T(8,128)(2,1)S(1)}, bf16[1,64,14336]{2,1,0:T(8,128)(2,1)}, u32[]{:S(2)}) copy-start(bf16[1,64,14336]{2,1,0:T(8,128)(2,1)} %local.15) | copy-start | bytes 5505028
  25.2 18.4 %collective-permute-start.8 = (bf16[64,1792]{1,0:T(8,128)(2,1)S(1)}, bf16[64,1792]{1,0:T(8,128)(2,1)S(1)}, u32[]{:S(2)}, u32[]{:S(2)}) collective-permute-start(bf16[64,1792]{1,0:T(8,128)(2,1)S(1)} %get-tuple-element.47), channel_id=1, source_target_pairs={{0,128},{128,0},{64,192},{192,64},{1,129},{129,1},{65,193},{193,65... | collective-permute-start | bytes 688136 | tf_op jit(solution)/shard_map/ppermute | solution.py:290
  34.7 1.9 %collective-permute-start.15 = (f32[64,512]{1,0:T(8,128)S(1)}, f32[64,512]{1,0:T(8,128)S(1)}, u32[]{:S(2)}, u32[]{:S(2)}) collective-permute-start(f32[64,512]{1,0:T(8,128)S(1)} %get-tuple-element.52.refs_4_), channel_id=1, source_target_pairs={{0,64},{64,0},{128,192},{192,128},{1,65},{65,1},{129,193},{193,129... | collective-permute-start | bytes 393224 | tf_op jit(solution)/shard_map/ppermute | solution.py:287
  35.6 10.0 %collective-permute-start.13 = (f32[64,640]{1,0:T(8,128)S(1)}, f32[64,640]{1,0:T(8,128)S(1)}, u32[]{:S(2)}, u32[]{:S(2)}) collective-permute-start(f32[64,640]{1,0:T(8,128)S(1)} %get-tuple-element.50.refs_2_), channel_id=1, source_target_pairs={{0,64},{64,0},{128,192},{192,128},{1,65},{65,1},{129,193},{193,129... | collective-permute-start | bytes 491528 | tf_op jit(solution)/shard_map/ppermute | solution.py:287
  35.7 10.0 %collective-permute-start.14 = (f32[64,640]{1,0:T(8,128)S(1)}, f32[64,640]{1,0:T(8,128)S(1)}, u32[]{:S(2)}, u32[]{:S(2)}) collective-permute-start(f32[64,640]{1,0:T(8,128)S(1)} %get-tuple-element.51.refs_3_), channel_id=1, source_target_pairs={{0,64},{64,0},{128,192},{192,128},{1,65},{65,1},{129,193},{193,129... | collective-permute-start | bytes 491528 | tf_op jit(solution)/shard_map/ppermute | solution.py:287
  36.1 12.0 %collective-permute-start.12 = (f32[64,768]{1,0:T(8,128)S(1)}, f32[64,768]{1,0:T(8,128)S(1)}, u32[]{:S(2)}, u32[]{:S(2)}) collective-permute-start(f32[64,768]{1,0:T(8,128)S(1)} %get-tuple-element.49.refs_1_), channel_id=1, source_target_pairs={{0,64},{64,0},{128,192},{192,128},{1,65},{65,1},{129,193},{193,129... | collective-permute-start | bytes 589832 | tf_op jit(solution)/shard_map/ppermute | solution.py:287
  36.6 14.8 %collective-permute-start.7 = (bf16[64,1792]{1,0:T(8,128)(2,1)S(1)}, bf16[64,1792]{1,0:T(8,128)(2,1)S(1)}, u32[]{:S(2)}, u32[]{:S(2)}) collective-permute-start(bf16[64,1792]{1,0:T(8,128)(2,1)S(1)} %get-tuple-element.46), channel_id=1, source_target_pairs={{0,128},{128,0},{64,192},{192,64},{1,129},{129,1},{65,193},{193,65... | collective-permute-start | bytes 688136 | tf_op jit(solution)/shard_map/ppermute | solution.py:290
  43.5 4.6 %collective-permute-start.11 = (f32[64,1024]{1,0:T(8,128)S(1)}, f32[64,1024]{1,0:T(8,128)S(1)}, u32[]{:S(2)}, u32[]{:S(2)}) collective-permute-start(f32[64,1024]{1,0:T(8,128)S(1)} %get-tuple-element.48.refs_0_), channel_id=1, source_target_pairs={{0,64},{64,0},{128,192},{192,128},{1,65},{65,1},{129,193},{193,129... | collective-permute-start | bytes 786440 | tf_op jit(solution)/shard_map/ppermute | solution.py:287
  45.6 4.6 %collective-permute-start.10 = (bf16[64,896]{1,0:T(8,128)(2,1)S(1)}, bf16[64,896]{1,0:T(8,128)(2,1)S(1)}, u32[]{:S(2)}, u32[]{:S(2)}) collective-permute-start(bf16[64,896]{1,0:T(8,128)(2,1)S(1)} %get-tuple-element.67), channel_id=1, source_target_pairs={{0,64},{64,0},{128,192},{192,128},{1,65},{65,1},{129,193},{193,129... | collective-permute-start | bytes 344072 | tf_op jit(solution)/shard_map/ppermute | solution.py:287
  45.7 4.5 %collective-permute-start.9 = (bf16[64,896]{1,0:T(8,128)(2,1)S(1)}, bf16[64,896]{1,0:T(8,128)(2,1)S(1)}, u32[]{:S(2)}, u32[]{:S(2)}) collective-permute-start(bf16[64,896]{1,0:T(8,128)(2,1)S(1)} %get-tuple-element.68), channel_id=1, source_target_pairs={{0,64},{64,0},{128,192},{192,128},{1,65},{65,1},{129,193},{193,129... | collective-permute-start | bytes 344072 | tf_op jit(solution)/shard_map/ppermute | solution.py:287
  51.4 1.9 %collective-permute-start.16 = (bf16[64,1792]{1,0:T(8,128)(2,1)S(1)}, bf16[64,1792]{1,0:T(8,128)(2,1)S(1)}, u32[]{:S(2)}, u32[]{:S(2)}) collective-permute-start(bf16[64,1792]{1,0:T(8,128)(2,1)S(1)} %collective-permute-done.7.refs_0_), channel_id=1, source_target_pairs={{0,64},{64,0},{128,192},{192,128},{1,65},{65,1},{129,193},{193,129... | collective-permute-start | bytes 688136 | tf_op jit(solution)/shard_map/ppermute | solution.py:287
